TPU v7x, 512 devices: a whole 4x4x16 slice. The times are simulated.
512 devices in a mesh: dp: 64 (over x, z_lo, core), fsdp: 8 (over y, z_hi).
Axes of the slice: x: 4, y: 4, z: 16 (z_hi: 2, z_lo: 8; z = z_hi * 8 + z_lo), core: 2. Of those that a mesh axis runs over, the one named last changes fastest.
Arguments:
- acts: bfloat16 [24576, 8192], P('dp', 'fsdp'), may hold values from -6 to 6
- grad_out: bfloat16 [24576, 8192], P('dp', 'fsdp'), may hold values from -16 to 16
- basis: bfloat16 [8192, 1024], P('fsdp', 'dp'), may hold values from -0.0625 to 0.0625
- master: float32 [8, 1024, 8192], P(None, 'dp', 'fsdp'), may hold values from -4 to 4
- first_mom: float32 [8, 1024, 1024], P('fsdp', 'dp'), may hold values from -2 to 2
- second_mom: float32 [8, 1024, 1024], P('fsdp', 'dp'), may hold values from 0.0001 to 0.01
Outputs:
- new_master: float32 [8, 1024, 8192], P(None, 'dp', 'fsdp')
- forward: bfloat16 [8, 1024, 8192], P(None, 'dp')
- new_first: float32 [8, 1024, 1024], P('fsdp', 'dp')
- new_second: float32 [8, 1024, 1024], P('fsdp', 'dp')
All inputs are finite; a program needn't handle non-finite values.
Results may differ from a plain program's by a relative error of at most 0.0021.
Values may be sent and summed in bfloat16 or wider, within the bound.
No kernel may reach another device: no remote copies, remote signals or barrier semaphores. Data moves between devices by JAX's collectives and lax.ppermute only.
A program may use at most 64 MiB of HBM per device.

v0:
```python
import math

import jax
import jax.numpy as jnp
from jax import lax
from jax.sharding import PartitionSpec as P

beta_one = 0.9
beta_two = 0.999
bias_first = 1.0 - 0.9**10
bias_second = 1.0 - 0.999**10
adam_eps = 1e-08
learn_rate = 0.1


def on_device(acts, grad_out, basis, master, first_mom, second_mom):
    data_count = lax.axis_size("dp")
    rank_full = basis.shape[1] * data_count
    basis_rows = lax.all_gather(basis, "dp", axis=1, tiled=True)
    partial_value = jnp.dot(acts, basis_rows, preferred_element_type=jnp.float32)
    projected = lax.psum(partial_value, "fsdp").astype(jnp.bfloat16)
    grad_scale = 1.0 / math.sqrt(acts.shape[0] * data_count)
    whole = lax.dot_general(
        grad_out, projected, (((0,), (0,)), ((), ())), preferred_element_type=jnp.float32
    )
    reduced = lax.psum_scatter(whole, "dp", scatter_dimension=0, tiled=True)
    grad = (reduced * grad_scale).reshape(first_mom.shape)
    new_first = beta_one * first_mom + (1.0 - beta_one) * grad
    new_second = beta_two * second_mom + (1.0 - beta_two) * grad * grad
    update = (new_first / bias_first / (jnp.sqrt(new_second / bias_second) + adam_eps)).astype(
        jnp.bfloat16
    )
    gathered = lax.all_gather(update, "fsdp", axis=0, tiled=True)
    flat_update = gathered.reshape(gathered.shape[0] * gathered.shape[1], rank_full)
    delta = lax.dot_general(
        flat_update, basis_rows, (((1,), (1,)), ((), ())), preferred_element_type=jnp.float32
    )
    new_master = master - learn_rate * delta.reshape(master.shape)
    forward = lax.all_gather(new_master.astype(jnp.bfloat16), "fsdp", axis=2, tiled=True)
    return (new_master, forward, new_first, new_second)


def solution(mesh):
    placed = (
        P("dp", "fsdp"),
        P("dp", "fsdp"),
        P("fsdp", "dp"),
        P(None, "dp", "fsdp"),
        P("fsdp", "dp", None),
        P("fsdp", "dp", None),
    )
    return jax.shard_map(
        on_device,
        mesh=mesh,
        in_specs=placed,
        out_specs=(
            P(None, "dp", "fsdp"),
            P(None, "dp", None),
            P("fsdp", "dp", None),
            P("fsdp", "dp", None),
        ),
        check_vma=False,
    )
```

profile of v0, /device:TPU:1, one launch (start us, length us, event | category | flops | bytes accessed | tf_op | source)
XLA Modules:
  0.0 1068.6 jit_solution(120360031509470938)
XLA Ops:
  7.2 0.0 copy-start
  7.2 0.0 all-gather.3.cloned.1.call-start
  7.2 0.7 all-gather.3.cloned.1.call-update
  7.9 0.0 reduce-scatter.4.cloned.1.call-start
  8.0 128.6 %all-gather.3.cloned.1.call-done = bf16[1024,1024]{0,1:T(8,128)(2,1)} async-done(((bf16[1024,16]{0,1:T(8,128)(2,1)}), bf16[1024,1024]{0,1:T(8,128)(2,1)}) %all-gather.3.cloned.1.call-update) | async-done | bytes 2097168 | tf_op jit(solution)/shard_map/all_gather | solution.py:19
  136.6 2.9 fusion.10
  139.4 258.9 %all-reduce.1 = bf16[384,1024]{1,0:T(8,128)(2,1)S(1)} all-reduce(f32[384,1024]{1,0:T(8,128)S(1)} %fusion.10), channel_id=1, replica_groups=mesh['dp'=64,'fsdp'=8] {'fsdp'}, use_global_device_ids=true, to_apply=%region_0.0 | all-reduce | flops 393216 | bytes 2359296 | tf_op jit(solution)/shard_map/psum | solution.py:21
  398.3 0.0 copy-done
  398.3 3.3 convolution_bitcast_fusion
  401.6 5.4 copy.27
  406.9 0.0 copy-start.3
  407.0 0.0 copy-start.4
  407.0 0.0 copy-start.1
  407.0 0.0 copy-start.2
  407.0 0.0 reduce-scatter.4.cloned.1.call-update
  407.0 0.0 all-gather.5.cloned.1.call-start
  407.0 466.7 %reduce-scatter.4.cloned.1.call-done = f32[16,1024]{1,0:T(8,128)} async-done(((f32[1024,1024]{1,0:T(8,128)}), f32[16,1024]{1,0:T(8,128)}) %reduce-scatter.4.cloned.1.call-update) | async-done | bytes 65552 | tf_op jit(solution)/shard_map/reduce_scatter | solution.py:26
  873.7 0.0 copy-done.3
  873.7 0.0 copy-done.4
  873.7 1.5 divide_convert_fusion
  875.2 59.1 %all_gather.10 = bf16[8,16,1024]{2,1,0:T(8,128)(2,1)S(1)} all-gather(bf16[1,16,1024]{2,1,0:T(8,128)(2,1)S(1)} %get-tuple-element.12), channel_id=1, replica_groups=mesh['dp'=64,'fsdp'=8] {'fsdp'}, dimensions={0}, use_global_device_ids=true | all-gather | bytes 294912 | tf_op jit(solution)/shard_map/all_gather | solution.py:33
  934.3 0.0 copy-done.1
  934.3 0.0 copy-done.2
  934.3 1.3 fusion.9
  935.7 0.0 all-gather.5.cloned.1.call-update
  935.7 123.2 %all-gather.5.cloned.1.call-done = bf16[8,16,8192]{2,1,0:T(8,128)(2,1)} async-done(((bf16[8,16,1024]{2,1,0:T(8,128)(2,1)}), bf16[8,16,8192]{2,1,0:T(8,128)(2,1)}) %all-gather.5.cloned.1.call-update) | async-done | bytes 2097168 | tf_op jit(solution)/shard_map/all_gather | solution.py:39
  1058.9 3.1 copy.32
Async XLA Ops:
  7.2 391.2 %copy-start = (bf16[384,1024]{1,0:T(8,128)(2,1)S(1)}, bf16[384,1024]{1,0:T(8,128)(2,1)}, u32[]{:S(2)}) copy-start(bf16[384,1024]{1,0:T(8,128)(2,1)} %param.7) | copy-start | bytes 2359300
  7.2 129.4 %all-gather.3.cloned.1.call-start = ((), (), s32[]{:S(2)}) async-start(), calls=%async_computation.1 | async-start | bytes 2129920 | tf_op jit(solution)/shard_map/all_gather | solution.py:19
  7.9 865.8 %reduce-scatter.4.cloned.1.call-start = ((), (), s32[]{:S(2)}) async-start(), calls=%async_computation.3 | async-start | bytes 4259840 | tf_op jit(solution)/shard_map/reduce_scatter | solution.py:26
  406.9 466.7 %copy-start.3 = (f32[1,16,1024]{2,1,0:T(8,128)S(1)}, f32[1,16,1024]{2,1,0:T(8,128)}, u32[]{:S(2)}) copy-start(f32[1,16,1024]{2,1,0:T(8,128)} %param.10) | copy-start | bytes 196612
  407.0 466.7 %copy-start.4 = (f32[1,16,1024]{2,1,0:T(8,128)S(1)}, f32[1,16,1024]{2,1,0:T(8,128)}, u32[]{:S(2)}) copy-start(f32[1,16,1024]{2,1,0:T(8,128)} %param.11) | copy-start | bytes 196612
  407.0 527.4 %copy-start.1 = (bf16[1024,1024]{0,1:T(8,128)(2,1)S(1)}, bf16[1024,1024]{0,1:T(8,128)(2,1)}, u32[]{:S(2)}) copy-start(bf16[1024,1024]{0,1:T(8,128)(2,1)} %all-gather.3.cloned.1.call-done) | copy-start | bytes 6291460
  407.0 527.4 %copy-start.2 = (f32[8,16,1024]{2,1,0:T(8,128)S(1)}, f32[8,16,1024]{2,1,0:T(8,128)}, u32[]{:S(2)}) copy-start(f32[8,16,1024]{2,1,0:T(8,128)} %param.9) | copy-start | bytes 1572868
  407.0 651.9 %all-gather.5.cloned.1.call-start = ((), (), s32[]{:S(2)}) async-start(), calls=%async_computation.2 | async-start | bytes 2359296 | tf_op jit(solution)/shard_map/all_gather | solution.py:39
Sparse Core Ops, SparseCore 0:
  10.2 126.3 all-gather.2
  407.1 466.5 reduce-scatter.3
  935.8 123.0 all-gather.4
where the time goes:
time: 1070 us
  waiting for transfers between devices  719 us (67%)
  blocking collectives  318 us (30%)
  between operations  13.8 us (1%)
    reduce_scatter x1, waiting for transfers between devices, on_device(): reduced = lax.psum_scatter(whole, 'dp', scatter_dimension=0, tiled=True)  467 us
    psum x1, blocking collectives, on_device(): projected = lax.psum(partial_value, 'fsdp').astype(jnp.bfloat16)  259 us
    all_gather x1, waiting for transfers between devices, on_device(): basis_rows = lax.all_gather(basis, 'dp', axis=1, tiled=True)  129 us
    all_gather x1, waiting for transfers between devices, on_device(): lax.all_gather(new_master.astype(jnp.bfloat16), 'fsdp', axis=2, tiled=True)  123 us
    all_gather x1, blocking collectives, on_device(): gathered = lax.all_gather(update, 'fsdp', axis=0, tiled=True)  59.1 us
  transfers between devices with their start and end apart: 3, of which 3 were waited for; matrix products, arithmetic and copies ran while one was open for 0% of the time, Pallas kernels for 0%

commit v1 on v0

v1 whole, which is shorter than its diff:
```python
import math

import jax
import jax.numpy as jnp
from jax import lax
from jax.sharding import Mesh
from jax.sharding import PartitionSpec as P

beta_one = 0.9
beta_two = 0.999
bias_first = 1.0 - 0.9**10
bias_second = 1.0 - 0.999**10
adam_eps = 1e-08
learn_rate = 0.1

bf16 = jnp.bfloat16
f16 = jnp.float16
f32 = jnp.float32

X, ZL, C, Y, ZH = 4, 8, 2, 4, 2
SWAP = [(0, 1), (1, 0)]


def encode(value):
    return (value * lax.rsqrt(jnp.abs(value) + 1e-30)).astype(f16)


def decode(coded):
    root = coded.astype(f32)
    return root * jnp.abs(root)


def swap(value, axis):
    return lax.ppermute(value, axis, SWAP)


def exchange(value, axis):
    return lax.all_to_all(value, axis, 0, 0)


def gather(value, axis, count):
    return exchange(jnp.broadcast_to(value[None], (count, *value.shape)), axis)


def ordered(first, other, at):
    return jnp.where(at == 0, first, other), jnp.where(at == 0, other, first)


def on_device(acts, grad_out, basis, master, first_mom, second_mom):
    core = lax.axis_index("c")
    high = lax.axis_index("zh")
    tokens = acts.shape[0] * X * ZL * C
    feats = acts.shape[1]
    cols = first_mom.shape[1]
    rank = first_mom.shape[2]
    half = rank // C
    part_rank = basis.shape[1]
    grad_scale = 1.0 / math.sqrt(tokens)

    acts_chip = jnp.concatenate([acts, swap(acts, "c")], 0)
    grad_out_chip = jnp.concatenate([grad_out, swap(grad_out, "c")], 0)

    rows = gather(basis.T, "zl", ZL).reshape(ZL * part_rank, feats)
    rows = gather(rows, "x", X).reshape(half, feats)
    rows_other = swap(rows, "c")

    partial_value = lax.dot_general(
        acts_chip, rows, (((1,), (1,)), ((), ())), preferred_element_type=f32
    )
    quarter = partial_value.shape[0] // Y
    coded = exchange(encode(partial_value).reshape(Y, quarter, half), "y")
    summed = decode(coded).sum(0)
    summed = summed + decode(swap(encode(summed), "zh"))
    projected = gather(summed.astype(bf16), "y", Y).reshape(Y * quarter, half)

    whole = lax.dot_general(
        grad_out_chip, projected, (((0,), (0,)), ((), ())), preferred_element_type=f32
    )
    whole = whole * grad_scale
    block = whole.shape[0] // X
    summed = decode(exchange(encode(whole).reshape(X, block, half), "x")).sum(0)
    coded = exchange(encode(summed).reshape(ZL * C, cols, half), ("zl", "c"))
    grad = decode(coded).reshape(ZL, C, cols, half).sum(0)
    grad = jnp.concatenate([grad[0], grad[1]], 1)

    at = lax.broadcasted_iota(jnp.int32, (rank, rank), 1)
    source = (at % half) // part_rank * (part_rank * C) + at // half * part_rank + at % part_rank
    by_core = (lax.broadcasted_iota(jnp.int32, (rank, rank), 0) == source).astype(f32)

    def permuted(value, dim):
        return lax.dot_general(
            value,
            by_core,
            (((1,), (dim,)), ((), ())),
            precision=lax.Precision.HIGHEST,
            preferred_element_type=f32,
        )

    moments = permuted(jnp.concatenate([first_mom[0], second_mom[0]], 0), 0)
    first = beta_one * moments[:cols] + (1.0 - beta_one) * grad
    second = beta_two * moments[cols:] + (1.0 - beta_two) * grad * grad
    update = (first / bias_first / (jnp.sqrt(second / bias_second) + adam_eps)).astype(bf16)
    moments = permuted(jnp.concatenate([first, second], 0), 1)
    new_first = moments[None, :cols]
    new_second = moments[None, cols:]

    rows_low, rows_high = ordered(rows, rows_other, core)
    rows_all = jnp.concatenate([rows_low, rows_high], 0)
    blocks = master.reshape(Y, ZH, cols, feats)
    master_near, master_far = ordered(blocks[:, 0], blocks[:, 1], high)

    def stepped(updates, old):
        delta = jnp.dot(updates.reshape(Y * cols, rank), rows_all, preferred_element_type=f32)
        new = old.reshape(Y * cols, feats) - learn_rate * delta
        return new, new.astype(bf16)

    update_far = swap(update, "zh")
    near, near_forward = stepped(gather(update, "y", Y), master_near)
    near_of_far = swap(near_forward, "zh")
    far, far_forward = stepped(gather(update_far, "y", Y), master_far)
    far_of_far = swap(far_forward, "zh")

    low, up = ordered(near.reshape(Y, cols, feats), far.reshape(Y, cols, feats), high)
    new_master = jnp.stack([low, up], 1).reshape(master.shape)

    own = gather(jnp.concatenate([near_forward, far_forward], 0), "y", Y)
    own = own.reshape(Y, ZH, Y, cols, feats)
    theirs_far = gather(near_of_far, "y", Y).reshape(Y, Y, cols, feats)
    theirs_near = gather(far_of_far, "y", Y).reshape(Y, Y, cols, feats)
    own_near, own_far = own[:, 0], own[:, 1]
    zero_zero, one_one = ordered(own_near, theirs_far, high)
    one_zero, zero_one = ordered(own_far, theirs_near, high)
    table = jnp.stack(
        [jnp.stack([zero_zero, zero_one], 0), jnp.stack([one_zero, one_one], 0)], 0
    )
    forward = table.transpose(3, 0, 4, 2, 1, 5).reshape(
        master.shape[0], cols, Y * ZH * feats
    )
    return (new_master, forward, new_first, new_second)


def solution(mesh):
    devices = mesh.devices.reshape(X, ZL, C, Y, ZH)
    fine = Mesh(devices, ("x", "zl", "c", "y", "zh"))
    dp = ("x", "zl", "c")
    fsdp = ("y", "zh")
    return jax.shard_map(
        on_device,
        mesh=fine,
        in_specs=(
            P(dp, fsdp),
            P(dp, fsdp),
            P(fsdp, dp),
            P(None, dp, fsdp),
            P(fsdp, dp, None),
            P(fsdp, dp, None),
        ),
        out_specs=(
            P(None, dp, fsdp),
            P(None, dp, None),
            P(fsdp, dp, None),
            P(fsdp, dp, None),
        ),
        check_vma=False,
    )
```

time: 1070 us -> 280 us (0.26)
  the two profiles are of different devices: /device:TPU:1 before, /device:TPU:64 now
where the time goes in v1:
time: 280 us; the launch traced here: 278 us
  waiting for transfers between devices  132 us (47%)
  starting transfers between devices  93.4 us (33%)
  local copies, waits for them, and re-layouts  15 us (5%)
  blocking collectives  13.9 us (5%)
  matrix products  13.7 us (5%)
  other arithmetic  8.72 us (3%)
    all_to_all x10, waiting for transfers between devices, exchange(): return lax.all_to_all(value, axis, 0, 0)  82.7 us
    all_to_all x10, starting transfers between devices, exchange(): return lax.all_to_all(value, axis, 0, 0)  59.3 us
    ppermute x7, waiting for transfers between devices, swap(): return lax.ppermute(value, axis, SWAP)  49.8 us
    ppermute x7, starting transfers between devices, swap(): return lax.ppermute(value, axis, SWAP)  34.1 us
    all_to_all x1, blocking collectives, exchange(): return lax.all_to_all(value, axis, 0, 0)  13.9 us
    broadcast_in_dim x8, local copies, waits for them, and re-layouts, gather(): return exchange(jnp.broadcast_to(value[None], (count, *value.shape)), axis)  8.48 us
  transfers between devices with their start and end apart: 17, of which 13 were waited for; matrix products, arithmetic and copies ran while one was open for 6% of the time, Pallas kernels for 0%

profile of v1, /device:TPU:64, one launch (start us, length us, event | category | flops | bytes accessed | tf_op | source)
XLA Modules:
  0.0 278.2 jit_solution(11277779080218314044)
XLA Ops:
  0.6 1.6 broadcast_in_dim.22
  2.2 12.2 %all-to-all-start = ((bf16[8,16,1024]{2,1,0:T(8,128)(2,1)}), bf16[8,16,1024]{2,1,0:T(8,128)(2,1)S(1)}, u32[]{:S(2)}, u32[]{:S(2)}) async-start(bf16[8,16,1024]{2,1,0:T(8,128)(2,1)} %broadcast_in_dim.22), calls=%async_computation | async-start | bytes 524288 | tf_op jit(solution)/shard_map/all_to_all | solution.py:38
  14.4 1.9 collective-permute-start.1
  16.3 13.1 %all-to-all-done = bf16[8,16,1024]{2,1,0:T(8,128)(2,1)S(1)} async-done(((bf16[8,16,1024]{2,1,0:T(8,128)(2,1)}), bf16[8,16,1024]{2,1,0:T(8,128)(2,1)S(1)}, u32[]{:S(2)}, u32[]{:S(2)}) %all-to-all-start) | async-done | bytes 262176 | tf_op jit(solution)/shard_map/all_to_all | solution.py:38
  29.4 1.1 broadcast_in_dim.24
  30.5 4.3 %all-to-all-start.1 = ((bf16[4,128,1024]{2,1,0:T(8,128)(2,1)}), bf16[4,128,1024]{2,1,0:T(8,128)(2,1)S(1)}, u32[]{:S(2)}, u32[]{:S(2)}) async-start(bf16[4,128,1024]{2,1,0:T(8,128)(2,1)} %broadcast_in_dim.24), calls=%async_computation.1 | async-start | bytes 2097152 | tf_op jit(solution)/shard_map/all_to_all | solution.py:38
  34.8 12.9 %all-to-all-done.1 = bf16[4,128,1024]{2,1,0:T(8,128)(2,1)S(1)} async-done(((bf16[4,128,1024]{2,1,0:T(8,128)(2,1)}), bf16[4,128,1024]{2,1,0:T(8,128)(2,1)S(1)}, u32[]{:S(2)}, u32[]{:S(2)}) %all-to-all-start.1) | async-done | bytes 1048608 | tf_op jit(solution)/shard_map/all_to_all | solution.py:38
  47.7 2.3 multiply_convert_fusion.1
  50.0 13.9 %all_to_all.55 = f16[4,192,512]{2,1,0:T(8,128)(2,1)S(1)} all-to-all(f16[4,192,512]{2,1,0:T(8,128)(2,1)S(1)} %bitcast.76), channel_id=1, replica_groups=mesh['x'=4,'zl'=8,'c'=2,'y'=4,'zh'=2] {'y'}, dimensions={0} | all-to-all | bytes 1572864 | tf_op jit(solution)/shard_map/all_to_all | solution.py:38
  63.8 0.2 fusion.10
  64.1 0.1 multiply_convert_fusion.3
  64.2 8.2 %collective-permute-start.2 = (f16[192,512]{1,0:T(8,128)(2,1)S(1)}, f16[192,512]{1,0:T(8,128)(2,1)S(1)}, u32[]{:S(2)}, u32[]{:S(2)}) collective-permute-start(f16[192,512]{1,0:T(8,128)(2,1)S(1)} %multiply_convert_fusion.3), channel_id=1, source_target_pairs={{0,1},{1,0},{2,3},{3,2},{4,5},{5,4},{6,7},{7,6},{8,9},{9,8},{10,11... | collective-permute-start | bytes 589832 | tf_op jit(solution)/shard_map/ppermute | solution.py:34
  72.4 1.9 collective-permute-start
  74.3 14.1 %collective-permute-done.2 = f16[192,512]{1,0:T(8,128)(2,1)S(1)} collective-permute-done((f16[192,512]{1,0:T(8,128)(2,1)S(1)}, f16[192,512]{1,0:T(8,128)(2,1)S(1)}, u32[]{:S(2)}, u32[]{:S(2)}) %collective-permute-start.2) | collective-permute-done | bytes 196640 | tf_op jit(solution)/shard_map/ppermute | solution.py:34
  88.5 0.9 broadcast_in_dim.25
  89.4 3.5 %all-to-all-start.3 = ((bf16[4,192,512]{2,1,0:T(8,128)(2,1)}), bf16[4,192,512]{2,1,0:T(8,128)(2,1)S(1)}, u32[]{:S(2)}, u32[]{:S(2)}) async-start(bf16[4,192,512]{2,1,0:T(8,128)(2,1)} %broadcast_in_dim.25), calls=%async_computation.3 | async-start | bytes 1572864 | tf_op jit(solution)/shard_map/all_to_all | solution.py:38
  92.9 9.4 %all-to-all-done.3 = bf16[4,192,512]{2,1,0:T(8,128)(2,1)S(1)} async-done(((bf16[4,192,512]{2,1,0:T(8,128)(2,1)}), bf16[4,192,512]{2,1,0:T(8,128)(2,1)S(1)}, u32[]{:S(2)}, u32[]{:S(2)}) %all-to-all-start.3) | async-done | bytes 786464 | tf_op jit(solution)/shard_map/all_to_all | solution.py:38
  102.4 3.4 %multiply_convert_fusion = f16[1024,512]{1,0:T(8,128)(2,1)} fusion(bf16[768,512]{1,0:T(8,128)(2,1)S(1)} %bitcast.75, bf16[384,1024]{1,0:T(8,128)(2,1)} %collective-permute-done, bf16[384,1024]{1,0:T(8,128)(2,1)S(1)} %copy-done.12), kind=kOutput, calls=%fused_computation.21 | convolution fusion | flops 811073536 | bytes 3407872 | tf_op jit(solution)/shard_map/dot_general | solution.py:76
  105.8 3.5 %all-to-all-start.4 = ((f16[4,256,512]{2,1,0:T(8,128)(2,1)}), f16[4,256,512]{2,1,0:T(8,128)(2,1)S(1)}, u32[]{:S(2)}, u32[]{:S(2)}) async-start(f16[4,256,512]{2,1,0:T(8,128)(2,1)} %bitcast.9), calls=%async_computation.4 | async-start | bytes 2097152 | tf_op jit(solution)/shard_map/all_to_all | solution.py:38
  109.4 10.8 %all-to-all-done.4 = f16[4,256,512]{2,1,0:T(8,128)(2,1)S(1)} async-done(((f16[4,256,512]{2,1,0:T(8,128)(2,1)}), f16[4,256,512]{2,1,0:T(8,128)(2,1)S(1)}, u32[]{:S(2)}, u32[]{:S(2)}) %all-to-all-start.4) | async-done | bytes 1048608 | tf_op jit(solution)/shard_map/all_to_all | solution.py:38
  120.2 0.3 fusion.9
  120.5 0.8 multiply_convert_fusion.2
  121.3 16.3 %all-to-all-start.5 = ((f16[16,16,512]{2,1,0:T(8,128)(2,1)}), f16[16,16,512]{2,1,0:T(8,128)(2,1)S(1)}, u32[]{:S(2)}, u32[]{:S(2)}) async-start(f16[16,16,512]{2,1,0:T(8,128)(2,1)} %multiply_convert_fusion.2), calls=%async_computation.5 | async-start | bytes 524288 | tf_op jit(solution)/shard_map/all_to_all | solution.py:38
  137.6 0.8 fusion.4
  138.3 2.1 collective-permute-start.3
  140.4 1.3 fusion.30
  141.8 10.9 %all-to-all-done.5 = f16[16,16,512]{2,1,0:T(8,128)(2,1)S(1)} async-done(((f16[16,16,512]{2,1,0:T(8,128)(2,1)}), f16[16,16,512]{2,1,0:T(8,128)(2,1)S(1)}, u32[]{:S(2)}, u32[]{:S(2)}) %all-to-all-start.5) | async-done | bytes 262176 | tf_op jit(solution)/shard_map/all_to_all | solution.py:38
  152.6 0.1 abs_multiply_fusion.2
  152.8 0.7 divide_convert_fusion
  153.4 6.7 %collective-permute-start.4 = (bf16[16,1024]{1,0:T(8,128)(2,1)S(1)}, bf16[16,1024]{1,0:T(8,128)(2,1)S(1)}, u32[]{:S(2)}, u32[]{:S(2)}) collective-permute-start(bf16[16,1024]{1,0:T(8,128)(2,1)S(1)} %get-tuple-element.4), channel_id=1, source_target_pairs={{0,1},{1,0},{2,3},{3,2},{4,5},{5,4},{6,7},{7,6},{8,9},{9,8},{10,11... | collective-permute-start | bytes 98312 | tf_op jit(solution)/shard_map/ppermute | solution.py:34
  160.1 0.8 fusion.29
  161.0 7.3 %collective-permute-done.4 = bf16[16,1024]{1,0:T(8,128)(2,1)S(1)} collective-permute-done((bf16[16,1024]{1,0:T(8,128)(2,1)S(1)}, bf16[16,1024]{1,0:T(8,128)(2,1)S(1)}, u32[]{:S(2)}, u32[]{:S(2)}) %collective-permute-start.4) | collective-permute-done | bytes 32800 | tf_op jit(solution)/shard_map/ppermute | solution.py:34
  168.2 0.7 broadcast_in_dim.27
  168.9 3.3 %all-to-all-start.7 = ((bf16[4,16,1024]{2,1,0:T(8,128)(2,1)}), bf16[4,16,1024]{2,1,0:T(8,128)(2,1)S(1)}, u32[]{:S(2)}, u32[]{:S(2)}) async-start(bf16[4,16,1024]{2,1,0:T(8,128)(2,1)} %broadcast_in_dim.27), calls=%async_computation.7 | async-start | bytes 262144 | tf_op jit(solution)/shard_map/all_to_all | solution.py:38
  172.3 2.4 broadcast_select_fusion.1
  174.6 3.5 %all-to-all-done.7 = bf16[4,16,1024]{2,1,0:T(8,128)(2,1)S(1)} async-done(((bf16[4,16,1024]{2,1,0:T(8,128)(2,1)}), bf16[4,16,1024]{2,1,0:T(8,128)(2,1)S(1)}, u32[]{:S(2)}, u32[]{:S(2)}) %all-to-all-start.7) | async-done | bytes 131104 | tf_op jit(solution)/shard_map/all_to_all | solution.py:38
  178.2 1.4 broadcast_in_dim.26
  179.6 4.0 %all-to-all-start.6 = ((bf16[4,16,1024]{2,1,0:T(8,128)(2,1)}), bf16[4,16,1024]{2,1,0:T(8,128)(2,1)}, u32[]{:S(2)}, u32[]{:S(2)}) async-start(bf16[4,16,1024]{2,1,0:T(8,128)(2,1)} %broadcast_in_dim.26), calls=%async_computation.6 | async-start | bytes 262144 | tf_op jit(solution)/shard_map/all_to_all | solution.py:38
  183.6 2.4 fusion.25
  186.0 3.6 %all-to-all-done.6 = bf16[4,16,1024]{2,1,0:T(8,128)(2,1)} async-done(((bf16[4,16,1024]{2,1,0:T(8,128)(2,1)}), bf16[4,16,1024]{2,1,0:T(8,128)(2,1)}, u32[]{:S(2)}, u32[]{:S(2)}) %all-to-all-start.6) | async-done | bytes 131104 | tf_op jit(solution)/shard_map/all_to_all | solution.py:38
  189.6 2.4 broadcast_select_fusion.7
  192.0 6.7 %collective-permute-start.5 = (bf16[64,1024]{1,0:T(8,128)(2,1)S(1)}, bf16[64,1024]{1,0:T(8,128)(2,1)S(1)}, u32[]{:S(2)}, u32[]{:S(2)}) collective-permute-start(bf16[64,1024]{1,0:T(8,128)(2,1)S(1)} %get-tuple-element.20), channel_id=1, source_target_pairs={{0,1},{1,0},{2,3},{3,2},{4,5},{5,4},{6,7},{7,6},{8,9},{9,8},{10,11... | collective-permute-start | bytes 393224 | tf_op jit(solution)/shard_map/ppermute | solution.py:34
  198.7 15.5 %collective-permute-done.5 = bf16[64,1024]{1,0:T(8,128)(2,1)S(1)} collective-permute-done((bf16[64,1024]{1,0:T(8,128)(2,1)S(1)}, bf16[64,1024]{1,0:T(8,128)(2,1)S(1)}, u32[]{:S(2)}, u32[]{:S(2)}) %collective-permute-start.5) | collective-permute-done | bytes 131104 | tf_op jit(solution)/shard_map/ppermute | solution.py:34
  214.1 0.9 broadcast_in_dim.29
  215.0 3.6 %all-to-all-start.9 = ((bf16[4,64,1024]{2,1,0:T(8,128)(2,1)}), bf16[4,64,1024]{2,1,0:T(8,128)(2,1)S(1)}, u32[]{:S(2)}, u32[]{:S(2)}) async-start(bf16[4,64,1024]{2,1,0:T(8,128)(2,1)} %broadcast_in_dim.29), calls=%async_computation.9 | async-start | bytes 1048576 | tf_op jit(solution)/shard_map/all_to_all | solution.py:38
  218.6 6.7 %collective-permute-start.6 = (bf16[64,1024]{1,0:T(8,128)(2,1)S(1)}, bf16[64,1024]{1,0:T(8,128)(2,1)S(1)}, u32[]{:S(2)}, u32[]{:S(2)}) collective-permute-start(bf16[64,1024]{1,0:T(8,128)(2,1)S(1)} %get-tuple-element.19), channel_id=1, source_target_pairs={{0,1},{1,0},{2,3},{3,2},{4,5},{5,4},{6,7},{7,6},{8,9},{9,8},{10,11... | collective-permute-start | bytes 393224 | tf_op jit(solution)/shard_map/ppermute | solution.py:34
  225.3 12.9 %collective-permute-done.6 = bf16[64,1024]{1,0:T(8,128)(2,1)S(1)} collective-permute-done((bf16[64,1024]{1,0:T(8,128)(2,1)S(1)}, bf16[64,1024]{1,0:T(8,128)(2,1)S(1)}, u32[]{:S(2)}, u32[]{:S(2)}) %collective-permute-start.6) | collective-permute-done | bytes 131104 | tf_op jit(solution)/shard_map/ppermute | solution.py:34
  238.2 0.9 broadcast_in_dim.30
  239.1 5.0 %all-to-all-start.10 = ((bf16[4,64,1024]{2,1,0:T(8,128)(2,1)}), bf16[4,64,1024]{2,1,0:T(8,128)(2,1)S(1)}, u32[]{:S(2)}, u32[]{:S(2)}) async-start(bf16[4,64,1024]{2,1,0:T(8,128)(2,1)} %broadcast_in_dim.30), calls=%async_computation.10 | async-start | bytes 1048576 | tf_op jit(solution)/shard_map/all_to_all | solution.py:38
  244.1 1.0 pad_maximum_fusion.12
  245.0 8.7 %all-to-all-done.10 = bf16[4,64,1024]{2,1,0:T(8,128)(2,1)S(1)} async-done(((bf16[4,64,1024]{2,1,0:T(8,128)(2,1)}), bf16[4,64,1024]{2,1,0:T(8,128)(2,1)S(1)}, u32[]{:S(2)}, u32[]{:S(2)}) %all-to-all-start.10) | async-done | bytes 524320 | tf_op jit(solution)/shard_map/all_to_all | solution.py:38
  253.7 1.1 broadcast_in_dim.28
  254.8 3.7 %all-to-all-start.8 = ((bf16[4,128,1024]{2,1,0:T(8,128)(2,1)}), bf16[4,128,1024]{2,1,0:T(8,128)(2,1)S(1)}, u32[]{:S(2)}, u32[]{:S(2)}) async-start(bf16[4,128,1024]{2,1,0:T(8,128)(2,1)} %broadcast_in_dim.28), calls=%async_computation.8 | async-start | bytes 2097152 | tf_op jit(solution)/shard_map/all_to_all | solution.py:38
  258.5 1.9 fusion.34
  260.4 0.7 slice_bitcast_fusion.4
  261.1 1.0 pad_maximum_fusion.11
  262.1 0.8 copy.23
  262.9 9.8 %all-to-all-done.8 = bf16[4,128,1024]{2,1,0:T(8,128)(2,1)S(1)} async-done(((bf16[4,128,1024]{2,1,0:T(8,128)(2,1)}), bf16[4,128,1024]{2,1,0:T(8,128)(2,1)S(1)}, u32[]{:S(2)}, u32[]{:S(2)}) %all-to-all-start.8) | async-done | bytes 1048608 | tf_op jit(solution)/shard_map/all_to_all | solution.py:38
  272.7 0.1 broadcast_select_fusion.5
  272.8 0.1 maximum_bitcast_fusion.1
  272.9 0.1 maximum_bitcast_fusion.2
  273.1 0.2 maximum_bitcast_fusion
  273.3 2.2 copy.24
  275.4 2.8 %reshape.187 = bf16[8,16,8192]{2,1,0:T(8,128)(2,1)} reshape(bf16[4,2,16,4,2,1024]{5,4,3,2,1,0:T(2,128)(2,1)S(1)} %copy.24) | data formatting | bytes 4194304 | tf_op jit(solution)/shard_map/reshape | solution.py:136
  (40 shorter events, 0.2 us)
Async XLA Ops:
  0.6 47.1 %copy-start.11 = (bf16[384,1024]{1,0:T(8,128)(2,1)S(1)}, bf16[384,1024]{1,0:T(8,128)(2,1)}, u32[]{:S(2)}) copy-start(bf16[384,1024]{1,0:T(8,128)(2,1)} %param.6) | copy-start | bytes 2359300
  2.2 27.2 %all-to-all-start = ((bf16[8,16,1024]{2,1,0:T(8,128)(2,1)}), bf16[8,16,1024]{2,1,0:T(8,128)(2,1)S(1)}, u32[]{:S(2)}, u32[]{:S(2)}) async-start(bf16[8,16,1024]{2,1,0:T(8,128)(2,1)} %broadcast_in_dim.22), calls=%async_computation | async-start | bytes 524288 | tf_op jit(solution)/shard_map/all_to_all | solution.py:38
  14.4 20.4 %collective-permute-start.1 = (bf16[384,1024]{1,0:T(8,128)(2,1)}, bf16[384,1024]{1,0:T(8,128)(2,1)S(1)}, u32[]{:S(2)}, u32[]{:S(2)}) collective-permute-start(bf16[384,1024]{1,0:T(8,128)(2,1)} %param.6), channel_id=1, source_target_pairs={{0,8},{8,0},{1,9},{9,1},{2,10},{10,2},{3,11},{11,3},{4,12},{12,4},... | collective-permute-start | bytes 2359304 | tf_op jit(solution)/shard_map/ppermute | solution.py:34
  30.5 17.2 %all-to-all-start.1 = ((bf16[4,128,1024]{2,1,0:T(8,128)(2,1)}), bf16[4,128,1024]{2,1,0:T(8,128)(2,1)S(1)}, u32[]{:S(2)}, u32[]{:S(2)}) async-start(bf16[4,128,1024]{2,1,0:T(8,128)(2,1)} %broadcast_in_dim.24), calls=%async_computation.1 | async-start | bytes 2097152 | tf_op jit(solution)/shard_map/all_to_all | solution.py:38
  34.8 12.9 %copy-start.13 = (bf16[384,1024]{1,0:T(8,128)(2,1)}, bf16[384,1024]{1,0:T(8,128)(2,1)S(1)}, u32[]{:S(2)}) copy-start(bf16[384,1024]{1,0:T(8,128)(2,1)S(1)} %collective-permute-done.1) | copy-start | bytes 2359300
  50.0 22.4 %copy-start.12 = (bf16[384,1024]{1,0:T(8,128)(2,1)S(1)}, bf16[384,1024]{1,0:T(8,128)(2,1)}, u32[]{:S(2)}) copy-start(bf16[384,1024]{1,0:T(8,128)(2,1)} %param.7) | copy-start | bytes 2359300
  64.2 24.3 %collective-permute-start.2 = (f16[192,512]{1,0:T(8,128)(2,1)S(1)}, f16[192,512]{1,0:T(8,128)(2,1)S(1)}, u32[]{:S(2)}, u32[]{:S(2)}) collective-permute-start(f16[192,512]{1,0:T(8,128)(2,1)S(1)} %multiply_convert_fusion.3), channel_id=1, source_target_pairs={{0,1},{1,0},{2,3},{3,2},{4,5},{5,4},{6,7},{7,6},{8,9},{9,8},{10,11... | collective-permute-start | bytes 589832 | tf_op jit(solution)/shard_map/ppermute | solution.py:34
  72.4 20.5 %collective-permute-start = (bf16[384,1024]{1,0:T(8,128)(2,1)S(1)}, bf16[384,1024]{1,0:T(8,128)(2,1)}, u32[]{:S(2)}, u32[]{:S(2)}) collective-permute-start(bf16[384,1024]{1,0:T(8,128)(2,1)S(1)} %copy-done.12), channel_id=1, source_target_pairs={{0,8},{8,0},{1,9},{9,1},{2,10},{10,2},{3,11},{11,3},{4,12},{12,4},... | collective-permute-start | bytes 2359304 | tf_op jit(solution)/shard_map/ppermute | solution.py:34
  89.4 13.0 %all-to-all-start.3 = ((bf16[4,192,512]{2,1,0:T(8,128)(2,1)}), bf16[4,192,512]{2,1,0:T(8,128)(2,1)S(1)}, u32[]{:S(2)}, u32[]{:S(2)}) async-start(bf16[4,192,512]{2,1,0:T(8,128)(2,1)} %broadcast_in_dim.25), calls=%async_computation.3 | async-start | bytes 1572864 | tf_op jit(solution)/shard_map/all_to_all | solution.py:38
  105.8 14.4 %all-to-all-start.4 = ((f16[4,256,512]{2,1,0:T(8,128)(2,1)}), f16[4,256,512]{2,1,0:T(8,128)(2,1)S(1)}, u32[]{:S(2)}, u32[]{:S(2)}) async-start(f16[4,256,512]{2,1,0:T(8,128)(2,1)} %bitcast.9), calls=%async_computation.4 | async-start | bytes 2097152 | tf_op jit(solution)/shard_map/all_to_all | solution.py:38
  109.3 31.1 %copy-start.9 = (f32[1,16,1024]{2,1,0:T(8,128)S(1)}, f32[1,16,1024]{2,1,0:T(8,128)}, u32[]{:S(2)}) copy-start(f32[1,16,1024]{2,1,0:T(8,128)} %param.11) | copy-start | bytes 196612
  109.3 31.1 %copy-start.10 = (f32[1,16,1024]{2,1,0:T(8,128)S(1)}, f32[1,16,1024]{2,1,0:T(8,128)}, u32[]{:S(2)}) copy-start(f32[1,16,1024]{2,1,0:T(8,128)} %param.10) | copy-start | bytes 196612
  121.3 31.3 %all-to-all-start.5 = ((f16[16,16,512]{2,1,0:T(8,128)(2,1)}), f16[16,16,512]{2,1,0:T(8,128)(2,1)S(1)}, u32[]{:S(2)}, u32[]{:S(2)}) async-start(f16[16,16,512]{2,1,0:T(8,128)(2,1)} %multiply_convert_fusion.2), calls=%async_computation.5 | async-start | bytes 524288 | tf_op jit(solution)/shard_map/all_to_all | solution.py:38
  137.6 22.6 %copy-start.1 = (f32[8,16,1024]{2,1,0:T(8,128)S(1)}, f32[8,16,1024]{2,1,0:T(8,128)}, u32[]{:S(2)}) copy-start(f32[8,16,1024]{2,1,0:T(8,128)} %param.9) | copy-start | bytes 1572868
  138.3 33.9 %collective-permute-start.3 = (bf16[512,1024]{1,0:T(8,128)(2,1)S(1)}, bf16[512,1024]{1,0:T(8,128)(2,1)}, u32[]{:S(2)}, u32[]{:S(2)}) collective-permute-start(bf16[512,1024]{1,0:T(8,128)(2,1)S(1)} %bitcast.68), channel_id=1, source_target_pairs={{0,8},{8,0},{1,9},{9,1},{2,10},{10,2},{3,11},{11,3},{4,12},{12,4},... | collective-permute-start | bytes 3145736 | tf_op jit(solution)/shard_map/ppermute | solution.py:34
  153.4 18.8 %copy-start.8 = (bf16[16,1024]{1,0:T(8,128)(2,1)}, bf16[16,1024]{1,0:T(8,128)(2,1)S(1)}, u32[]{:S(2)}) copy-start(bf16[16,1024]{1,0:T(8,128)(2,1)S(1)} %get-tuple-element.4) | copy-start | bytes 98308
  153.4 14.8 %collective-permute-start.4 = (bf16[16,1024]{1,0:T(8,128)(2,1)S(1)}, bf16[16,1024]{1,0:T(8,128)(2,1)S(1)}, u32[]{:S(2)}, u32[]{:S(2)}) collective-permute-start(bf16[16,1024]{1,0:T(8,128)(2,1)S(1)} %get-tuple-element.4), channel_id=1, source_target_pairs={{0,1},{1,0},{2,3},{3,2},{4,5},{5,4},{6,7},{7,6},{8,9},{9,8},{10,11... | collective-permute-start | bytes 98312 | tf_op jit(solution)/shard_map/ppermute | solution.py:34
  168.9 9.3 %all-to-all-start.7 = ((bf16[4,16,1024]{2,1,0:T(8,128)(2,1)}), bf16[4,16,1024]{2,1,0:T(8,128)(2,1)S(1)}, u32[]{:S(2)}, u32[]{:S(2)}) async-start(bf16[4,16,1024]{2,1,0:T(8,128)(2,1)} %broadcast_in_dim.27), calls=%async_computation.7 | async-start | bytes 262144 | tf_op jit(solution)/shard_map/all_to_all | solution.py:38
  172.2 11.3 %copy-start.4 = (f32[4,1,16,1024]{3,2,0,1:T(8,128)S(1)}, f32[4,1,16,1024]{3,2,0,1:T(8,128)}, u32[]{:S(2)}) copy-start(f32[4,1,16,1024]{3,2,0,1:T(8,128)} %get-tuple-element.18) | copy-start | bytes 786436
  174.6 14.9 %copy-start = (bf16[512,1024]{1,0:T(8,128)(2,1)S(1)}, bf16[512,1024]{1,0:T(8,128)(2,1)}, u32[]{:S(2)}) copy-start(bf16[512,1024]{1,0:T(8,128)(2,1)} %get-tuple-element.8) | copy-start | bytes 3145732
  179.6 10.0 %all-to-all-start.6 = ((bf16[4,16,1024]{2,1,0:T(8,128)(2,1)}), bf16[4,16,1024]{2,1,0:T(8,128)(2,1)}, u32[]{:S(2)}, u32[]{:S(2)}) async-start(bf16[4,16,1024]{2,1,0:T(8,128)(2,1)} %broadcast_in_dim.26), calls=%async_computation.6 | async-start | bytes 262144 | tf_op jit(solution)/shard_map/all_to_all | solution.py:38
  192.0 22.2 %copy-start.6 = (bf16[64,1024]{1,0:T(8,128)(2,1)}, bf16[64,1024]{1,0:T(8,128)(2,1)S(1)}, u32[]{:S(2)}) copy-start(bf16[64,1024]{1,0:T(8,128)(2,1)S(1)} %get-tuple-element.20) | copy-start | bytes 393220
  192.0 47.1 %copy-start.5 = (bf16[64,1024]{1,0:T(8,128)(2,1)}, bf16[64,1024]{1,0:T(8,128)(2,1)S(1)}, u32[]{:S(2)}) copy-start(bf16[64,1024]{1,0:T(8,128)(2,1)S(1)} %get-tuple-element.19) | copy-start | bytes 393220
  192.0 22.1 %collective-permute-start.5 = (bf16[64,1024]{1,0:T(8,128)(2,1)S(1)}, bf16[64,1024]{1,0:T(8,128)(2,1)S(1)}, u32[]{:S(2)}, u32[]{:S(2)}) collective-permute-start(bf16[64,1024]{1,0:T(8,128)(2,1)S(1)} %get-tuple-element.20), channel_id=1, source_target_pairs={{0,1},{1,0},{2,3},{3,2},{4,5},{5,4},{6,7},{7,6},{8,9},{9,8},{10,11... | collective-permute-start | bytes 393224 | tf_op jit(solution)/shard_map/ppermute | solution.py:34
  215.0 29.1 %copy-start.7 = (bf16[64,1024]{1,0:T(8,128)(2,1)S(1)}, bf16[64,1024]{1,0:T(8,128)(2,1)}, u32[]{:S(2)}) copy-start(bf16[64,1024]{1,0:T(8,128)(2,1)} %copy-done.6) | copy-start | bytes 393220
  215.0 23.2 %all-to-all-start.9 = ((bf16[4,64,1024]{2,1,0:T(8,128)(2,1)}), bf16[4,64,1024]{2,1,0:T(8,128)(2,1)S(1)}, u32[]{:S(2)}, u32[]{:S(2)}) async-start(bf16[4,64,1024]{2,1,0:T(8,128)(2,1)} %broadcast_in_dim.29), calls=%async_computation.9 | async-start | bytes 1048576 | tf_op jit(solution)/shard_map/all_to_all | solution.py:38
  218.6 19.6 %collective-permute-start.6 = (bf16[64,1024]{1,0:T(8,128)(2,1)S(1)}, bf16[64,1024]{1,0:T(8,128)(2,1)S(1)}, u32[]{:S(2)}, u32[]{:S(2)}) collective-permute-start(bf16[64,1024]{1,0:T(8,128)(2,1)S(1)} %get-tuple-element.19), channel_id=1, source_target_pairs={{0,1},{1,0},{2,3},{3,2},{4,5},{5,4},{6,7},{7,6},{8,9},{9,8},{10,11... | collective-permute-start | bytes 393224 | tf_op jit(solution)/shard_map/ppermute | solution.py:34
  239.1 14.6 %all-to-all-start.10 = ((bf16[4,64,1024]{2,1,0:T(8,128)(2,1)}), bf16[4,64,1024]{2,1,0:T(8,128)(2,1)S(1)}, u32[]{:S(2)}, u32[]{:S(2)}) async-start(bf16[4,64,1024]{2,1,0:T(8,128)(2,1)} %broadcast_in_dim.30), calls=%async_computation.10 | async-start | bytes 1048576 | tf_op jit(solution)/shard_map/all_to_all | solution.py:38
  244.1 14.5 %copy-start.2 = (f32[16,1024]{1,0:T(8,128)S(1)}, f32[16,1024]{1,0:T(8,128)}, u32[]{:S(2)}) copy-start(f32[16,1024]{1,0:T(8,128)} %get-tuple-element.5) | copy-start | bytes 196612
  244.1 14.5 %copy-start.3 = (f32[16,1024]{1,0:T(8,128)S(1)}, f32[16,1024]{1,0:T(8,128)}, u32[]{:S(2)}) copy-start(f32[16,1024]{1,0:T(8,128)} %get-tuple-element.6) | copy-start | bytes 196612
  254.8 17.9 %all-to-all-start.8 = ((bf16[4,128,1024]{2,1,0:T(8,128)(2,1)}), bf16[4,128,1024]{2,1,0:T(8,128)(2,1)S(1)}, u32[]{:S(2)}, u32[]{:S(2)}) async-start(bf16[4,128,1024]{2,1,0:T(8,128)(2,1)} %broadcast_in_dim.28), calls=%async_computation.8 | async-start | bytes 2097152 | tf_op jit(solution)/shard_map/all_to_all | solution.py:38

commit v2 on v1

--- a/solution.py
+++ b/solution.py
@@ -18,6 +18,7 @@
 f32 = jnp.float32
 
 X, ZL, C, Y, ZH = 4, 8, 2, 4, 2
+ROWS = 8
 SWAP = [(0, 1), (1, 0)]
 
 
@@ -106,34 +107,27 @@
 
     rows_low, rows_high = ordered(rows, rows_other, core)
     rows_all = jnp.concatenate([rows_low, rows_high], 0)
-    blocks = master.reshape(Y, ZH, cols, feats)
-    master_near, master_far = ordered(blocks[:, 0], blocks[:, 1], high)
+    both = jnp.concatenate([update, swap(update, "zh")], 0)
+    updates = gather(both, "y", Y).reshape(Y, ZH, cols, rank)
+    low, up = ordered(updates[:, 0], updates[:, 1], high)
+    updates = jnp.stack([low, up], 1).reshape(Y * ZH * cols, rank)
+    delta = jnp.dot(updates, rows_all, preferred_element_type=f32)
+    new_master = master - learn_rate * delta.reshape(master.shape)
+    block_forward = new_master.astype(bf16).reshape(Y * ZH * cols, feats)
 
-    def stepped(updates, old):
-        delta = jnp.dot(updates.reshape(Y * cols, rank), rows_all, preferred_element_type=f32)
-        new = old.reshape(Y * cols, feats) - learn_rate * delta
-        return new, new.astype(bf16)
-
-    update_far = swap(update, "zh")
-    near, near_forward = stepped(gather(update, "y", Y), master_near)
-    near_of_far = swap(near_forward, "zh")
-    far, far_forward = stepped(gather(update_far, "y", Y), master_far)
-    far_of_far = swap(far_forward, "zh")
-
-    low, up = ordered(near.reshape(Y, cols, feats), far.reshape(Y, cols, feats), high)
-    new_master = jnp.stack([low, up], 1).reshape(master.shape)
-
-    own = gather(jnp.concatenate([near_forward, far_forward], 0), "y", Y)
-    own = own.reshape(Y, ZH, Y, cols, feats)
-    theirs_far = gather(near_of_far, "y", Y).reshape(Y, Y, cols, feats)
-    theirs_near = gather(far_of_far, "y", Y).reshape(Y, Y, cols, feats)
-    own_near, own_far = own[:, 0], own[:, 1]
-    zero_zero, one_one = ordered(own_near, theirs_far, high)
-    one_zero, zero_one = ordered(own_far, theirs_near, high)
-    table = jnp.stack(
-        [jnp.stack([zero_zero, zero_one], 0), jnp.stack([one_zero, one_one], 0)], 0
-    )
-    forward = table.transpose(3, 0, 4, 2, 1, 5).reshape(
+    tiled = (Y, Y * ZH, cols // ROWS, ROWS, feats)
+    here = lax.axis_index("y")
+    parts = [block_forward] + [
+        lax.ppermute(block_forward, "y", [(i, (i + d) % Y) for i in range(Y)]) for d in (2, 1, 3)
+    ]
+    far_block = swap(block_forward, "zh")
+    *parts, far_block = lax.optimization_barrier((*parts, far_block))
+    by_step = [parts[0], parts[2], parts[1], parts[3]]
+    stacked = jnp.stack(by_step[::-1] + by_step[::-1], 0)
+    own = lax.dynamic_slice_in_dim(stacked, Y - 1 - here, Y, 0)
+    theirs = gather(far_block, "y", Y).reshape(tiled)
+    forward = jnp.stack(ordered(own.reshape(tiled), theirs, high), 1)
+    forward = forward.transpose(2, 3, 4, 0, 1, 5).reshape(
         master.shape[0], cols, Y * ZH * feats
     )
     return (new_master, forward, new_first, new_second)

time: 280 us -> 239 us (0.85)
  the two profiles are of different devices: /device:TPU:64 before, /device:TPU:32 now
where the time goes in v2:
time: 239 us; the launch traced here: 238 us
  waiting for transfers between devices  108 us (45%)
  starting transfers between devices  86.3 us (36%)
  blocking collectives  13.9 us (6%)
  local copies, waits for them, and re-layouts  13.4 us (6%)
  matrix products  9.19 us (4%)
  other arithmetic  6.35 us (3%)
    all_to_all x7, waiting for transfers between devices, exchange(): return lax.all_to_all(value, axis, 0, 0)  71.1 us
    all_to_all x7, starting transfers between devices, exchange(): return lax.all_to_all(value, axis, 0, 0)  50.6 us
    ppermute x6, waiting for transfers between devices, swap(): return lax.ppermute(value, axis, SWAP)  36.8 us
    ppermute x6, starting transfers between devices, swap(): return lax.ppermute(value, axis, SWAP)  27.4 us
    all_to_all x1, blocking collectives, exchange(): return lax.all_to_all(value, axis, 0, 0)  13.9 us
    ppermute x3, starting transfers between devices, on_device(): lax.ppermute(block_forward, 'y', [(i, (i + d) % Y) for i in range(Y)])  8.37 us
    broadcast_in_dim x5, local copies, waits for them, and re-layouts, gather(): return exchange(jnp.broadcast_to(value[None], (count, *value.shape)), axis)  5.45 us
    unnamed x15, local copies, waits for them, and re-layouts  5.07 us
  transfers between devices with their start and end apart: 16, of which 10 were waited for; matrix products, arithmetic and copies ran while one was open for 7% of the time, Pallas kernels for 0%

profile of v2, /device:TPU:32, one launch (start us, length us, event | category | flops | bytes accessed | tf_op | source)
XLA Modules:
  0.0 238.0 jit_solution(1591123133516817100)
XLA Ops:
  0.6 0.0 copy-start.2
  0.6 1.6 broadcast_in_dim.16
  2.2 12.6 %all-to-all-start = ((bf16[8,16,1024]{2,1,0:T(8,128)(2,1)}), bf16[8,16,1024]{2,1,0:T(8,128)(2,1)S(1)}, u32[]{:S(2)}, u32[]{:S(2)}) async-start(bf16[8,16,1024]{2,1,0:T(8,128)(2,1)} %broadcast_in_dim.16), calls=%async_computation | async-start | bytes 524288 | tf_op jit(solution)/shard_map/all_to_all | solution.py:39
  14.8 1.9 collective-permute-start.1
  16.8 14.4 %all-to-all-done = bf16[8,16,1024]{2,1,0:T(8,128)(2,1)S(1)} async-done(((bf16[8,16,1024]{2,1,0:T(8,128)(2,1)}), bf16[8,16,1024]{2,1,0:T(8,128)(2,1)S(1)}, u32[]{:S(2)}, u32[]{:S(2)}) %all-to-all-start) | async-done | bytes 262176 | tf_op jit(solution)/shard_map/all_to_all | solution.py:39
  31.1 1.1 broadcast_in_dim.18
  32.2 4.3 %all-to-all-start.1 = ((bf16[4,128,1024]{2,1,0:T(8,128)(2,1)}), bf16[4,128,1024]{2,1,0:T(8,128)(2,1)S(1)}, u32[]{:S(2)}, u32[]{:S(2)}) async-start(bf16[4,128,1024]{2,1,0:T(8,128)(2,1)} %broadcast_in_dim.18), calls=%async_computation.1 | async-start | bytes 2097152 | tf_op jit(solution)/shard_map/all_to_all | solution.py:39
  36.5 0.0 collective-permute-done.1
  36.5 10.9 %all-to-all-done.1 = bf16[4,128,1024]{2,1,0:T(8,128)(2,1)S(1)} async-done(((bf16[4,128,1024]{2,1,0:T(8,128)(2,1)}), bf16[4,128,1024]{2,1,0:T(8,128)(2,1)S(1)}, u32[]{:S(2)}, u32[]{:S(2)}) %all-to-all-start.1) | async-done | bytes 1048608 | tf_op jit(solution)/shard_map/all_to_all | solution.py:39
  47.4 1.1 multiply_convert_fusion.1
  48.5 0.0 copy-start.3
  48.5 13.9 %all_to_all.40 = f16[4,192,512]{2,1,0:T(8,128)(2,1)S(1)} all-to-all(f16[4,192,512]{2,1,0:T(8,128)(2,1)S(1)} %bitcast.70), channel_id=1, replica_groups=mesh['x'=4,'zl'=8,'c'=2,'y'=4,'zh'=2] {'y'}, dimensions={0} | all-to-all | bytes 1572864 | tf_op jit(solution)/shard_map/all_to_all | solution.py:39
  62.4 0.2 fusion.13
  62.6 0.1 multiply_convert_fusion.3
  62.7 8.2 %collective-permute-start.2 = (f16[192,512]{1,0:T(8,128)(2,1)S(1)}, f16[192,512]{1,0:T(8,128)(2,1)S(1)}, u32[]{:S(2)}, u32[]{:S(2)}) collective-permute-start(f16[192,512]{1,0:T(8,128)(2,1)S(1)} %multiply_convert_fusion.3), channel_id=1, source_target_pairs={{0,1},{1,0},{2,3},{3,2},{4,5},{5,4},{6,7},{7,6},{8,9},{9,8},{10,11... | collective-permute-start | bytes 589832 | tf_op jit(solution)/shard_map/ppermute | solution.py:35
  71.0 1.9 collective-permute-start
  72.9 11.4 %collective-permute-done.2 = f16[192,512]{1,0:T(8,128)(2,1)S(1)} collective-permute-done((f16[192,512]{1,0:T(8,128)(2,1)S(1)}, f16[192,512]{1,0:T(8,128)(2,1)S(1)}, u32[]{:S(2)}, u32[]{:S(2)}) %collective-permute-start.2) | collective-permute-done | bytes 196640 | tf_op jit(solution)/shard_map/ppermute | solution.py:35
  84.3 0.1 fusion.26
  84.3 0.9 broadcast_in_dim.19
  85.3 3.5 %all-to-all-start.3 = ((bf16[4,192,512]{2,1,0:T(8,128)(2,1)}), bf16[4,192,512]{2,1,0:T(8,128)(2,1)S(1)}, u32[]{:S(2)}, u32[]{:S(2)}) async-start(bf16[4,192,512]{2,1,0:T(8,128)(2,1)} %broadcast_in_dim.19), calls=%async_computation.3 | async-start | bytes 1572864 | tf_op jit(solution)/shard_map/all_to_all | solution.py:39
  88.8 9.4 %all-to-all-done.3 = bf16[4,192,512]{2,1,0:T(8,128)(2,1)S(1)} async-done(((bf16[4,192,512]{2,1,0:T(8,128)(2,1)}), bf16[4,192,512]{2,1,0:T(8,128)(2,1)S(1)}, u32[]{:S(2)}, u32[]{:S(2)}) %all-to-all-start.3) | async-done | bytes 786464 | tf_op jit(solution)/shard_map/all_to_all | solution.py:39
  98.2 2.3 multiply_convert_fusion
  100.5 3.5 %all-to-all-start.4 = ((f16[4,256,512]{2,1,0:T(8,128)(2,1)}), f16[4,256,512]{2,1,0:T(8,128)(2,1)S(1)}, u32[]{:S(2)}, u32[]{:S(2)}) async-start(f16[4,256,512]{2,1,0:T(8,128)(2,1)} %bitcast.7), calls=%async_computation.4 | async-start | bytes 2097152 | tf_op jit(solution)/shard_map/all_to_all | solution.py:39
  104.0 0.0 copy-start
  104.0 0.0 copy-start.1
  104.1 1.9 collective-permute-start.4
  106.0 8.8 %all-to-all-done.4 = f16[4,256,512]{2,1,0:T(8,128)(2,1)S(1)} async-done(((f16[4,256,512]{2,1,0:T(8,128)(2,1)}), f16[4,256,512]{2,1,0:T(8,128)(2,1)S(1)}, u32[]{:S(2)}, u32[]{:S(2)}) %all-to-all-start.4) | async-done | bytes 1048608 | tf_op jit(solution)/shard_map/all_to_all | solution.py:39
  114.9 0.3 fusion.9
  115.2 0.8 multiply_convert_fusion.2
  116.0 19.7 %all-to-all-start.5 = ((f16[16,16,512]{2,1,0:T(8,128)(2,1)}), f16[16,16,512]{2,1,0:T(8,128)(2,1)S(1)}, u32[]{:S(2)}, u32[]{:S(2)}) async-start(f16[16,16,512]{2,1,0:T(8,128)(2,1)} %multiply_convert_fusion.2), calls=%async_computation.5 | async-start | bytes 524288 | tf_op jit(solution)/shard_map/all_to_all | solution.py:39
  135.7 0.8 fusion.4
  136.5 1.3 fusion.27
  137.8 12.2 %all-to-all-done.5 = f16[16,16,512]{2,1,0:T(8,128)(2,1)S(1)} async-done(((f16[16,16,512]{2,1,0:T(8,128)(2,1)}), f16[16,16,512]{2,1,0:T(8,128)(2,1)S(1)}, u32[]{:S(2)}, u32[]{:S(2)}) %all-to-all-start.5) | async-done | bytes 262176 | tf_op jit(solution)/shard_map/all_to_all | solution.py:39
  150.0 0.1 abs_multiply_fusion.2
  150.2 0.1 divide_convert_fusion
  150.2 6.7 %collective-permute-start.3 = (bf16[16,1024]{1,0:T(8,128)(2,1)S(1)}, bf16[16,1024]{1,0:T(8,128)(2,1)S(1)}, u32[]{:S(2)}, u32[]{:S(2)}) collective-permute-start(bf16[16,1024]{1,0:T(8,128)(2,1)S(1)} %get-tuple-element.14), channel_id=1, source_target_pairs={{0,1},{1,0},{2,3},{3,2},{4,5},{5,4},{6,7},{7,6},{8,9},{9,8},{10,11... | collective-permute-start | bytes 98312 | tf_op jit(solution)/shard_map/ppermute | solution.py:35
  156.9 7.8 %collective-permute-done.3 = bf16[16,1024]{1,0:T(8,128)(2,1)S(1)} collective-permute-done((bf16[16,1024]{1,0:T(8,128)(2,1)S(1)}, bf16[16,1024]{1,0:T(8,128)(2,1)S(1)}, u32[]{:S(2)}, u32[]{:S(2)}) %collective-permute-start.3) | collective-permute-done | bytes 32800 | tf_op jit(solution)/shard_map/ppermute | solution.py:35
  164.8 0.7 broadcast_in_dim.20
  165.5 3.4 %all-to-all-start.6 = ((bf16[4,32,1024]{2,1,0:T(8,128)(2,1)}), bf16[4,32,1024]{2,1,0:T(8,128)(2,1)S(1)}, u32[]{:S(2)}, u32[]{:S(2)}) async-start(bf16[4,32,1024]{2,1,0:T(8,128)(2,1)} %broadcast_in_dim.20), calls=%async_computation.6 | async-start | bytes 524288 | tf_op jit(solution)/shard_map/all_to_all | solution.py:39
  168.9 2.3 broadcast_select_fusion.3
  171.3 5.6 %all-to-all-done.6 = bf16[4,32,1024]{2,1,0:T(8,128)(2,1)S(1)} async-done(((bf16[4,32,1024]{2,1,0:T(8,128)(2,1)}), bf16[4,32,1024]{2,1,0:T(8,128)(2,1)S(1)}, u32[]{:S(2)}, u32[]{:S(2)}) %all-to-all-start.6) | async-done | bytes 262176 | tf_op jit(solution)/shard_map/all_to_all | solution.py:39
  177.0 2.6 %fusion.54 = (bf16[8,16,1024]{2,1,0:T(8,128)(2,1)S(1)}, f32[8,16,1024]{2,1,0:T(8,128)}) fusion(f32[8,16,1024]{2,1,0:T(8,128)} %param.9, bf16[8,16,1024]{2,1,0:T(8,128)(2,1)S(1)} %bitcast.71, bf16[512,1024]{1,0:T(8,128)(2,1)} %get-tuple-element.20, bf16[512,1024]{1,0:T(8,128)(2,1)S(1)} %get-tuple-element.19), kind=kOutput, calls=%fused_computation.97 | convolution fusion | flops 273022976 | bytes 3670016 | tf_op jit(solution)/shard_map/dot_general | solution.py:114
  179.6 6.7 %collective-permute-start.8 = (bf16[128,1024]{1,0:T(8,128)(2,1)S(1)}, bf16[128,1024]{1,0:T(8,128)(2,1)S(1)}, u32[]{:S(2)}, u32[]{:S(2)}) collective-permute-start(bf16[128,1024]{1,0:T(8,128)(2,1)S(1)} %bitcast.63), channel_id=1, source_target_pairs={{0,1},{1,0},{2,3},{3,2},{4,5},{5,4},{6,7},{7,6},{8,9},{9,8},{10,11... | collective-permute-start | bytes 786440 | tf_op jit(solution)/shard_map/ppermute | solution.py:35
  186.3 3.1 %collective-permute-start.7 = (bf16[128,1024]{1,0:T(8,128)(2,1)S(1)}, bf16[128,1024]{1,0:T(8,128)(2,1)S(1)}, u32[]{:S(2)}, u32[]{:S(2)}) collective-permute-start(bf16[128,1024]{1,0:T(8,128)(2,1)S(1)} %bitcast.64), channel_id=1, source_target_pairs={{0,6},{2,0},{4,2},{6,4},{1,7},{3,1},{5,3},{7,5},{8,14},{10,8},{12,... | collective-permute-start | bytes 786440 | tf_op jit(solution)/shard_map/ppermute | solution.py:121
  189.4 2.8 %collective-permute-start.6 = (bf16[128,1024]{1,0:T(8,128)(2,1)S(1)}, bf16[128,1024]{1,0:T(8,128)(2,1)S(1)}, u32[]{:S(2)}, u32[]{:S(2)}) collective-permute-start(bf16[128,1024]{1,0:T(8,128)(2,1)S(1)} %bitcast.65), channel_id=1, source_target_pairs={{0,2},{2,4},{4,6},{6,0},{1,3},{3,5},{5,7},{7,1},{8,10},{10,12},{12... | collective-permute-start | bytes 786440 | tf_op jit(solution)/shard_map/ppermute | solution.py:121
  192.1 2.5 %collective-permute-start.5 = (bf16[128,1024]{1,0:T(8,128)(2,1)S(1)}, bf16[128,1024]{1,0:T(8,128)(2,1)S(1)}, u32[]{:S(2)}, u32[]{:S(2)}) collective-permute-start(bf16[128,1024]{1,0:T(8,128)(2,1)S(1)} %bitcast.66), channel_id=1, source_target_pairs={{0,4},{2,6},{4,0},{6,2},{1,5},{3,7},{5,1},{7,3},{8,12},{10,14},{12... | collective-permute-start | bytes 786440 | tf_op jit(solution)/shard_map/ppermute | solution.py:121
  194.7 1.9 fusion.31
  196.5 0.7 slice_bitcast_fusion
  197.2 17.6 %collective-permute-done.8 = bf16[128,1024]{1,0:T(8,128)(2,1)S(1)} collective-permute-done((bf16[128,1024]{1,0:T(8,128)(2,1)S(1)}, bf16[128,1024]{1,0:T(8,128)(2,1)S(1)}, u32[]{:S(2)}, u32[]{:S(2)}) %collective-permute-start.8) | collective-permute-done | bytes 262176 | tf_op jit(solution)/shard_map/ppermute | solution.py:35
  214.8 0.0 collective-permute-done.7
  214.8 1.1 broadcast_in_dim.42
  215.9 3.5 %all-to-all-start.7 = ((bf16[4,128,1024]{2,1,0:T(8,128)(2,1)}), bf16[4,128,1024]{2,1,0:T(8,128)(2,1)S(1)}, u32[]{:S(2)}, u32[]{:S(2)}) async-start(bf16[4,128,1024]{2,1,0:T(8,128)(2,1)} %broadcast_in_dim.42), calls=%async_computation.7 | async-start | bytes 2097152 | tf_op jit(solution)/shard_map/all_to_all | solution.py:39
  219.4 0.7 bitcast_dynamic-update-slice_fusion.6
  220.2 0.7 bitcast_dynamic-update-slice_fusion.4
  220.9 0.7 bitcast_dynamic-update-slice_fusion.2
  221.6 0.7 bitcast_dynamic-update-slice_fusion
  222.3 0.7 bitcast_dynamic-update-slice_fusion.7
  223.1 0.7 bitcast_dynamic-update-slice_fusion.5
  223.8 0.7 bitcast_dynamic-update-slice_fusion.3
  224.5 0.7 bitcast_dynamic-update-slice_fusion.1
  225.2 9.7 %all-to-all-done.7 = bf16[4,128,1024]{2,1,0:T(8,128)(2,1)S(1)} async-done(((bf16[4,128,1024]{2,1,0:T(8,128)(2,1)}), bf16[4,128,1024]{2,1,0:T(8,128)(2,1)S(1)}, u32[]{:S(2)}, u32[]{:S(2)}) %all-to-all-start.7) | async-done | bytes 1048608 | tf_op jit(solution)/shard_map/all_to_all | solution.py:39
  234.9 1.4 broadcast_select_fusion.1
  236.3 0.2 pad_maximum_fusion
  236.5 1.5 copy.14
  (18 shorter events, 0.1 us)
Async XLA Ops:
  0.6 46.8 %copy-start.2 = (bf16[384,1024]{1,0:T(8,128)(2,1)S(1)}, bf16[384,1024]{1,0:T(8,128)(2,1)}, u32[]{:S(2)}) copy-start(bf16[384,1024]{1,0:T(8,128)(2,1)} %param.6) | copy-start | bytes 2359300
  2.2 28.9 %all-to-all-start = ((bf16[8,16,1024]{2,1,0:T(8,128)(2,1)}), bf16[8,16,1024]{2,1,0:T(8,128)(2,1)S(1)}, u32[]{:S(2)}, u32[]{:S(2)}) async-start(bf16[8,16,1024]{2,1,0:T(8,128)(2,1)} %broadcast_in_dim.16), calls=%async_computation | async-start | bytes 524288 | tf_op jit(solution)/shard_map/all_to_all | solution.py:39
  14.8 21.7 %collective-permute-start.1 = (bf16[384,1024]{1,0:T(8,128)(2,1)}, bf16[384,1024]{1,0:T(8,128)(2,1)S(1)}, u32[]{:S(2)}, u32[]{:S(2)}) collective-permute-start(bf16[384,1024]{1,0:T(8,128)(2,1)} %param.6), channel_id=1, source_target_pairs={{0,8},{8,0},{1,9},{9,1},{2,10},{10,2},{3,11},{11,3},{4,12},{12,4},... | collective-permute-start | bytes 2359304 | tf_op jit(solution)/shard_map/ppermute | solution.py:35
  32.2 15.2 %all-to-all-start.1 = ((bf16[4,128,1024]{2,1,0:T(8,128)(2,1)}), bf16[4,128,1024]{2,1,0:T(8,128)(2,1)S(1)}, u32[]{:S(2)}, u32[]{:S(2)}) async-start(bf16[4,128,1024]{2,1,0:T(8,128)(2,1)} %broadcast_in_dim.18), calls=%async_computation.1 | async-start | bytes 2097152 | tf_op jit(solution)/shard_map/all_to_all | solution.py:39
  48.5 22.4 %copy-start.3 = (bf16[384,1024]{1,0:T(8,128)(2,1)S(1)}, bf16[384,1024]{1,0:T(8,128)(2,1)}, u32[]{:S(2)}) copy-start(bf16[384,1024]{1,0:T(8,128)(2,1)} %param.7) | copy-start | bytes 2359300
  62.7 21.5 %collective-permute-start.2 = (f16[192,512]{1,0:T(8,128)(2,1)S(1)}, f16[192,512]{1,0:T(8,128)(2,1)S(1)}, u32[]{:S(2)}, u32[]{:S(2)}) collective-permute-start(f16[192,512]{1,0:T(8,128)(2,1)S(1)} %multiply_convert_fusion.3), channel_id=1, source_target_pairs={{0,1},{1,0},{2,3},{3,2},{4,5},{5,4},{6,7},{7,6},{8,9},{9,8},{10,11... | collective-permute-start | bytes 589832 | tf_op jit(solution)/shard_map/ppermute | solution.py:35
  71.0 17.8 %collective-permute-start = (bf16[384,1024]{1,0:T(8,128)(2,1)S(1)}, bf16[384,1024]{1,0:T(8,128)(2,1)S(1)}, u32[]{:S(2)}, u32[]{:S(2)}) collective-permute-start(bf16[384,1024]{1,0:T(8,128)(2,1)S(1)} %copy-done.3), channel_id=1, source_target_pairs={{0,8},{8,0},{1,9},{9,1},{2,10},{10,2},{3,11},{11,3},{4,12},{12,4},... | collective-permute-start | bytes 2359304 | tf_op jit(solution)/shard_map/ppermute | solution.py:35
  85.3 13.0 %all-to-all-start.3 = ((bf16[4,192,512]{2,1,0:T(8,128)(2,1)}), bf16[4,192,512]{2,1,0:T(8,128)(2,1)S(1)}, u32[]{:S(2)}, u32[]{:S(2)}) async-start(bf16[4,192,512]{2,1,0:T(8,128)(2,1)} %broadcast_in_dim.19), calls=%async_computation.3 | async-start | bytes 1572864 | tf_op jit(solution)/shard_map/all_to_all | solution.py:39
  100.5 14.4 %all-to-all-start.4 = ((f16[4,256,512]{2,1,0:T(8,128)(2,1)}), f16[4,256,512]{2,1,0:T(8,128)(2,1)S(1)}, u32[]{:S(2)}, u32[]{:S(2)}) async-start(f16[4,256,512]{2,1,0:T(8,128)(2,1)} %bitcast.7), calls=%async_computation.4 | async-start | bytes 2097152 | tf_op jit(solution)/shard_map/all_to_all | solution.py:39
  104.0 32.5 %copy-start = (f32[1,16,1024]{2,1,0:T(8,128)S(1)}, f32[1,16,1024]{2,1,0:T(8,128)}, u32[]{:S(2)}) copy-start(f32[1,16,1024]{2,1,0:T(8,128)} %param.11) | copy-start | bytes 196612
  104.0 32.5 %copy-start.1 = (f32[1,16,1024]{2,1,0:T(8,128)S(1)}, f32[1,16,1024]{2,1,0:T(8,128)}, u32[]{:S(2)}) copy-start(f32[1,16,1024]{2,1,0:T(8,128)} %param.10) | copy-start | bytes 196612
  104.1 64.8 %collective-permute-start.4 = (bf16[512,1024]{1,0:T(8,128)(2,1)S(1)}, bf16[512,1024]{1,0:T(8,128)(2,1)}, u32[]{:S(2)}, u32[]{:S(2)}) collective-permute-start(bf16[512,1024]{1,0:T(8,128)(2,1)S(1)} %bitcast.55), channel_id=1, source_target_pairs={{0,8},{8,0},{1,9},{9,1},{2,10},{10,2},{3,11},{11,3},{4,12},{12,4},... | collective-permute-start | bytes 3145736 | tf_op jit(solution)/shard_map/ppermute | solution.py:35
  116.0 34.0 %all-to-all-start.5 = ((f16[16,16,512]{2,1,0:T(8,128)(2,1)}), f16[16,16,512]{2,1,0:T(8,128)(2,1)S(1)}, u32[]{:S(2)}, u32[]{:S(2)}) async-start(f16[16,16,512]{2,1,0:T(8,128)(2,1)} %multiply_convert_fusion.2), calls=%async_computation.5 | async-start | bytes 524288 | tf_op jit(solution)/shard_map/all_to_all | solution.py:39
  150.2 14.5 %collective-permute-start.3 = (bf16[16,1024]{1,0:T(8,128)(2,1)S(1)}, bf16[16,1024]{1,0:T(8,128)(2,1)S(1)}, u32[]{:S(2)}, u32[]{:S(2)}) collective-permute-start(bf16[16,1024]{1,0:T(8,128)(2,1)S(1)} %get-tuple-element.14), channel_id=1, source_target_pairs={{0,1},{1,0},{2,3},{3,2},{4,5},{5,4},{6,7},{7,6},{8,9},{9,8},{10,11... | collective-permute-start | bytes 98312 | tf_op jit(solution)/shard_map/ppermute | solution.py:35
  165.5 11.4 %all-to-all-start.6 = ((bf16[4,32,1024]{2,1,0:T(8,128)(2,1)}), bf16[4,32,1024]{2,1,0:T(8,128)(2,1)S(1)}, u32[]{:S(2)}, u32[]{:S(2)}) async-start(bf16[4,32,1024]{2,1,0:T(8,128)(2,1)} %broadcast_in_dim.20), calls=%async_computation.6 | async-start | bytes 524288 | tf_op jit(solution)/shard_map/all_to_all | solution.py:39
  179.6 35.2 %collective-permute-start.8 = (bf16[128,1024]{1,0:T(8,128)(2,1)S(1)}, bf16[128,1024]{1,0:T(8,128)(2,1)S(1)}, u32[]{:S(2)}, u32[]{:S(2)}) collective-permute-start(bf16[128,1024]{1,0:T(8,128)(2,1)S(1)} %bitcast.63), channel_id=1, source_target_pairs={{0,1},{1,0},{2,3},{3,2},{4,5},{5,4},{6,7},{7,6},{8,9},{9,8},{10,11... | collective-permute-start | bytes 786440 | tf_op jit(solution)/shard_map/ppermute | solution.py:35
  186.3 28.5 %collective-permute-start.7 = (bf16[128,1024]{1,0:T(8,128)(2,1)S(1)}, bf16[128,1024]{1,0:T(8,128)(2,1)S(1)}, u32[]{:S(2)}, u32[]{:S(2)}) collective-permute-start(bf16[128,1024]{1,0:T(8,128)(2,1)S(1)} %bitcast.64), channel_id=1, source_target_pairs={{0,6},{2,0},{4,2},{6,4},{1,7},{3,1},{5,3},{7,5},{8,14},{10,8},{12,... | collective-permute-start | bytes 786440 | tf_op jit(solution)/shard_map/ppermute | solution.py:121
  189.4 25.4 %collective-permute-start.6 = (bf16[128,1024]{1,0:T(8,128)(2,1)S(1)}, bf16[128,1024]{1,0:T(8,128)(2,1)S(1)}, u32[]{:S(2)}, u32[]{:S(2)}) collective-permute-start(bf16[128,1024]{1,0:T(8,128)(2,1)S(1)} %bitcast.65), channel_id=1, source_target_pairs={{0,2},{2,4},{4,6},{6,0},{1,3},{3,5},{5,7},{7,1},{8,10},{10,12},{12... | collective-permute-start | bytes 786440 | tf_op jit(solution)/shard_map/ppermute | solution.py:121
  192.1 22.7 %collective-permute-start.5 = (bf16[128,1024]{1,0:T(8,128)(2,1)S(1)}, bf16[128,1024]{1,0:T(8,128)(2,1)S(1)}, u32[]{:S(2)}, u32[]{:S(2)}) collective-permute-start(bf16[128,1024]{1,0:T(8,128)(2,1)S(1)} %bitcast.66), channel_id=1, source_target_pairs={{0,4},{2,6},{4,0},{6,2},{1,5},{3,7},{5,1},{7,3},{8,12},{10,14},{12... | collective-permute-start | bytes 786440 | tf_op jit(solution)/shard_map/ppermute | solution.py:121
  215.9 19.0 %all-to-all-start.7 = ((bf16[4,128,1024]{2,1,0:T(8,128)(2,1)}), bf16[4,128,1024]{2,1,0:T(8,128)(2,1)S(1)}, u32[]{:S(2)}, u32[]{:S(2)}) async-start(bf16[4,128,1024]{2,1,0:T(8,128)(2,1)} %broadcast_in_dim.42), calls=%async_computation.7 | async-start | bytes 2097152 | tf_op jit(solution)/shard_map/all_to_all | solution.py:39

commit v3 on v2

--- a/solution.py
+++ b/solution.py
@@ -125,9 +125,15 @@
     by_step = [parts[0], parts[2], parts[1], parts[3]]
     stacked = jnp.stack(by_step[::-1] + by_step[::-1], 0)
     own = lax.dynamic_slice_in_dim(stacked, Y - 1 - here, Y, 0)
-    theirs = gather(far_block, "y", Y).reshape(tiled)
-    forward = jnp.stack(ordered(own.reshape(tiled), theirs, high), 1)
-    forward = forward.transpose(2, 3, 4, 0, 1, 5).reshape(
+    theirs = gather(far_block, "y", Y)
+
+    def tiles(block):
+        return block.reshape(tiled).transpose(1, 2, 0, 3, 4)[:, :, :, None]
+
+    table = jnp.zeros((Y * ZH, cols // ROWS, Y, ZH, ROWS, feats), bf16)
+    table = lax.dynamic_update_slice(table, tiles(own), (0, 0, 0, high, 0, 0))
+    table = lax.dynamic_update_slice(table, tiles(theirs), (0, 0, 0, 1 - high, 0, 0))
+    forward = table.transpose(0, 1, 4, 2, 3, 5).reshape(
         master.shape[0], cols, Y * ZH * feats
     )
     return (new_master, forward, new_first, new_second)

time: 239 us -> 237 us (level)
  local copies, waits for them, and re-layouts: 13.4 us -> 8.15 us
  waiting for transfers between devices: 108 us -> 113 us
    all_to_all x7, waiting for transfers between devices: 71.1 us -> 76.2 us  [exchange(): return lax.all_to_all(value, axis, 0, 0)]
    unnamed x15 -> x17, local copies, waits for them, and re-layouts: 5.07 us -> 1.47 us
  transfers between devices with their start and end apart: 16 -> 16, of which waited for: 10 -> 10; matrix products, arithmetic and copies ran while one was open for 7% -> 5% of each run, Pallas kernels for 0% -> 0%
where the time goes in v3:
time: 237 us; the launch traced here: 236 us
  waiting for transfers between devices  113 us (48%)
  starting transfers between devices  86.3 us (36%)
  blocking collectives  13.9 us (6%)
  matrix products  9.2 us (4%)
  local copies, waits for them, and re-layouts  8.15 us (3%)
  other arithmetic  4.79 us (2%)
    all_to_all x7, waiting for transfers between devices, exchange(): return lax.all_to_all(value, axis, 0, 0)  76.2 us
    all_to_all x7, starting transfers between devices, exchange(): return lax.all_to_all(value, axis, 0, 0)  50.6 us
    ppermute x6, waiting for transfers between devices, swap(): return lax.ppermute(value, axis, SWAP)  36.8 us
    ppermute x6, starting transfers between devices, swap(): return lax.ppermute(value, axis, SWAP)  27.4 us
    all_to_all x1, blocking collectives, exchange(): return lax.all_to_all(value, axis, 0, 0)  13.9 us
    ppermute x3, starting transfers between devices, on_device(): lax.ppermute(block_forward, 'y', [(i, (i + d) % Y) for i in range(Y)])  8.37 us
    broadcast_in_dim x5, local copies, waits for them, and re-layouts, gather(): return exchange(jnp.broadcast_to(value[None], (count, *value.shape)), axis)  5.43 us
  transfers between devices with their start and end apart: 16, of which 10 were waited for; matrix products, arithmetic and copies ran while one was open for 5% of the time, Pallas kernels for 0%

profile of v3, /device:TPU:32, one launch (start us, length us, event | category | flops | bytes accessed | tf_op | source)
XLA Modules:
  0.0 236.4 jit_solution(9318087298437587199)
XLA Ops:
  0.6 0.0 copy-start.3
  0.6 1.6 broadcast_in_dim.22
  2.2 12.6 %all-to-all-start = ((bf16[8,16,1024]{2,1,0:T(8,128)(2,1)}), bf16[8,16,1024]{2,1,0:T(8,128)(2,1)S(1)}, u32[]{:S(2)}, u32[]{:S(2)}) async-start(bf16[8,16,1024]{2,1,0:T(8,128)(2,1)} %broadcast_in_dim.22), calls=%async_computation | async-start | bytes 524288 | tf_op jit(solution)/shard_map/all_to_all | solution.py:39
  14.8 1.9 collective-permute-start.1
  16.8 14.4 %all-to-all-done = bf16[8,16,1024]{2,1,0:T(8,128)(2,1)S(1)} async-done(((bf16[8,16,1024]{2,1,0:T(8,128)(2,1)}), bf16[8,16,1024]{2,1,0:T(8,128)(2,1)S(1)}, u32[]{:S(2)}, u32[]{:S(2)}) %all-to-all-start) | async-done | bytes 262176 | tf_op jit(solution)/shard_map/all_to_all | solution.py:39
  31.1 1.1 broadcast_in_dim.48
  32.2 4.3 %all-to-all-start.1 = ((bf16[4,128,1024]{2,1,0:T(8,128)(2,1)}), bf16[4,128,1024]{2,1,0:T(8,128)(2,1)S(1)}, u32[]{:S(2)}, u32[]{:S(2)}) async-start(bf16[4,128,1024]{2,1,0:T(8,128)(2,1)} %broadcast_in_dim.48), calls=%async_computation.1 | async-start | bytes 2097152 | tf_op jit(solution)/shard_map/all_to_all | solution.py:39
  36.5 0.0 collective-permute-done.1
  36.5 10.9 %all-to-all-done.1 = bf16[4,128,1024]{2,1,0:T(8,128)(2,1)S(1)} async-done(((bf16[4,128,1024]{2,1,0:T(8,128)(2,1)}), bf16[4,128,1024]{2,1,0:T(8,128)(2,1)S(1)}, u32[]{:S(2)}, u32[]{:S(2)}) %all-to-all-start.1) | async-done | bytes 1048608 | tf_op jit(solution)/shard_map/all_to_all | solution.py:39
  47.4 0.0 copy-done.3
  47.4 1.1 multiply_convert_fusion.1
  48.5 0.0 copy-start.4
  48.5 13.9 %all_to_all.40 = f16[4,192,512]{2,1,0:T(8,128)(2,1)S(1)} all-to-all(f16[4,192,512]{2,1,0:T(8,128)(2,1)S(1)} %bitcast.78), channel_id=1, replica_groups=mesh['x'=4,'zl'=8,'c'=2,'y'=4,'zh'=2] {'y'}, dimensions={0} | all-to-all | bytes 1572864 | tf_op jit(solution)/shard_map/all_to_all | solution.py:39
  62.4 0.2 fusion.13
  62.6 0.1 multiply_convert_fusion.3
  62.7 8.2 %collective-permute-start.2 = (f16[192,512]{1,0:T(8,128)(2,1)S(1)}, f16[192,512]{1,0:T(8,128)(2,1)S(1)}, u32[]{:S(2)}, u32[]{:S(2)}) collective-permute-start(f16[192,512]{1,0:T(8,128)(2,1)S(1)} %multiply_convert_fusion.3), channel_id=1, source_target_pairs={{0,1},{1,0},{2,3},{3,2},{4,5},{5,4},{6,7},{7,6},{8,9},{9,8},{10,11... | collective-permute-start | bytes 589832 | tf_op jit(solution)/shard_map/ppermute | solution.py:35
  71.0 1.9 collective-permute-start
  72.9 11.4 %collective-permute-done.2 = f16[192,512]{1,0:T(8,128)(2,1)S(1)} collective-permute-done((f16[192,512]{1,0:T(8,128)(2,1)S(1)}, f16[192,512]{1,0:T(8,128)(2,1)S(1)}, u32[]{:S(2)}, u32[]{:S(2)}) %collective-permute-start.2) | collective-permute-done | bytes 196640 | tf_op jit(solution)/shard_map/ppermute | solution.py:35
  84.3 0.1 fusion.26
  84.3 0.9 broadcast_in_dim.49
  85.3 3.5 %all-to-all-start.3 = ((bf16[4,192,512]{2,1,0:T(8,128)(2,1)}), bf16[4,192,512]{2,1,0:T(8,128)(2,1)S(1)}, u32[]{:S(2)}, u32[]{:S(2)}) async-start(bf16[4,192,512]{2,1,0:T(8,128)(2,1)} %broadcast_in_dim.49), calls=%async_computation.3 | async-start | bytes 1572864 | tf_op jit(solution)/shard_map/all_to_all | solution.py:39
  88.8 0.0 collective-permute-done
  88.8 9.4 %all-to-all-done.3 = bf16[4,192,512]{2,1,0:T(8,128)(2,1)S(1)} async-done(((bf16[4,192,512]{2,1,0:T(8,128)(2,1)}), bf16[4,192,512]{2,1,0:T(8,128)(2,1)S(1)}, u32[]{:S(2)}, u32[]{:S(2)}) %all-to-all-start.3) | async-done | bytes 786464 | tf_op jit(solution)/shard_map/all_to_all | solution.py:39
  98.2 2.3 multiply_convert_fusion
  100.5 3.5 %all-to-all-start.4 = ((f16[4,256,512]{2,1,0:T(8,128)(2,1)}), f16[4,256,512]{2,1,0:T(8,128)(2,1)S(1)}, u32[]{:S(2)}, u32[]{:S(2)}) async-start(f16[4,256,512]{2,1,0:T(8,128)(2,1)} %bitcast.7), calls=%async_computation.4 | async-start | bytes 2097152 | tf_op jit(solution)/shard_map/all_to_all | solution.py:39
  104.0 0.0 copy-start.1
  104.0 0.0 copy-start.2
  104.1 1.9 collective-permute-start.4
  106.0 8.8 %all-to-all-done.4 = f16[4,256,512]{2,1,0:T(8,128)(2,1)S(1)} async-done(((f16[4,256,512]{2,1,0:T(8,128)(2,1)}), f16[4,256,512]{2,1,0:T(8,128)(2,1)S(1)}, u32[]{:S(2)}, u32[]{:S(2)}) %all-to-all-start.4) | async-done | bytes 1048608 | tf_op jit(solution)/shard_map/all_to_all | solution.py:39
  114.9 0.3 fusion.9
  115.2 0.8 multiply_convert_fusion.2
  116.0 19.7 %all-to-all-start.5 = ((f16[16,16,512]{2,1,0:T(8,128)(2,1)}), f16[16,16,512]{2,1,0:T(8,128)(2,1)S(1)}, u32[]{:S(2)}, u32[]{:S(2)}) async-start(f16[16,16,512]{2,1,0:T(8,128)(2,1)} %multiply_convert_fusion.2), calls=%async_computation.5 | async-start | bytes 524288 | tf_op jit(solution)/shard_map/all_to_all | solution.py:39
  135.7 0.8 fusion.4
  136.5 1.3 fusion.27
  137.8 12.2 %all-to-all-done.5 = f16[16,16,512]{2,1,0:T(8,128)(2,1)S(1)} async-done(((f16[16,16,512]{2,1,0:T(8,128)(2,1)}), f16[16,16,512]{2,1,0:T(8,128)(2,1)S(1)}, u32[]{:S(2)}, u32[]{:S(2)}) %all-to-all-start.5) | async-done | bytes 262176 | tf_op jit(solution)/shard_map/all_to_all | solution.py:39
  150.0 0.1 abs_multiply_fusion.2
  150.2 0.1 divide_convert_fusion
  150.2 6.7 %collective-permute-start.3 = (bf16[16,1024]{1,0:T(8,128)(2,1)S(1)}, bf16[16,1024]{1,0:T(8,128)(2,1)S(1)}, u32[]{:S(2)}, u32[]{:S(2)}) collective-permute-start(bf16[16,1024]{1,0:T(8,128)(2,1)S(1)} %get-tuple-element.14), channel_id=1, source_target_pairs={{0,1},{1,0},{2,3},{3,2},{4,5},{5,4},{6,7},{7,6},{8,9},{9,8},{10,11... | collective-permute-start | bytes 98312 | tf_op jit(solution)/shard_map/ppermute | solution.py:35
  156.9 7.8 %collective-permute-done.3 = bf16[16,1024]{1,0:T(8,128)(2,1)S(1)} collective-permute-done((bf16[16,1024]{1,0:T(8,128)(2,1)S(1)}, bf16[16,1024]{1,0:T(8,128)(2,1)S(1)}, u32[]{:S(2)}, u32[]{:S(2)}) %collective-permute-start.3) | collective-permute-done | bytes 32800 | tf_op jit(solution)/shard_map/ppermute | solution.py:35
  164.8 0.7 broadcast_in_dim.50
  165.5 3.4 %all-to-all-start.6 = ((bf16[4,32,1024]{2,1,0:T(8,128)(2,1)}), bf16[4,32,1024]{2,1,0:T(8,128)(2,1)S(1)}, u32[]{:S(2)}, u32[]{:S(2)}) async-start(bf16[4,32,1024]{2,1,0:T(8,128)(2,1)} %broadcast_in_dim.50), calls=%async_computation.6 | async-start | bytes 524288 | tf_op jit(solution)/shard_map/all_to_all | solution.py:39
  168.9 0.0 collective-permute-done.4
  168.9 2.3 broadcast_select_fusion.1
  171.3 5.6 %all-to-all-done.6 = bf16[4,32,1024]{2,1,0:T(8,128)(2,1)S(1)} async-done(((bf16[4,32,1024]{2,1,0:T(8,128)(2,1)}), bf16[4,32,1024]{2,1,0:T(8,128)(2,1)S(1)}, u32[]{:S(2)}, u32[]{:S(2)}) %all-to-all-start.6) | async-done | bytes 262176 | tf_op jit(solution)/shard_map/all_to_all | solution.py:39
  177.0 2.6 %fusion.54 = (bf16[8,16,1024]{2,1,0:T(8,128)(2,1)S(1)}, f32[8,16,1024]{2,1,0:T(8,128)}) fusion(f32[8,16,1024]{2,1,0:T(8,128)} %param.9, bf16[8,16,1024]{2,1,0:T(8,128)(2,1)S(1)} %bitcast.79, bf16[512,1024]{1,0:T(8,128)(2,1)} %get-tuple-element.18, bf16[512,1024]{1,0:T(8,128)(2,1)S(1)} %get-tuple-element.17), kind=kOutput, calls=%fused_computation.97 | convolution fusion | flops 273022976 | bytes 3670016 | tf_op jit(solution)/shard_map/dot_general | solution.py:114
  179.6 6.7 %collective-permute-start.8 = (bf16[128,1024]{1,0:T(8,128)(2,1)S(1)}, bf16[128,1024]{1,0:T(8,128)(2,1)S(1)}, u32[]{:S(2)}, u32[]{:S(2)}) collective-permute-start(bf16[128,1024]{1,0:T(8,128)(2,1)S(1)} %bitcast.71), channel_id=1, source_target_pairs={{0,1},{1,0},{2,3},{3,2},{4,5},{5,4},{6,7},{7,6},{8,9},{9,8},{10,11... | collective-permute-start | bytes 786440 | tf_op jit(solution)/shard_map/ppermute | solution.py:35
  186.3 3.1 %collective-permute-start.7 = (bf16[128,1024]{1,0:T(8,128)(2,1)S(1)}, bf16[128,1024]{1,0:T(8,128)(2,1)S(1)}, u32[]{:S(2)}, u32[]{:S(2)}) collective-permute-start(bf16[128,1024]{1,0:T(8,128)(2,1)S(1)} %bitcast.72), channel_id=1, source_target_pairs={{0,6},{2,0},{4,2},{6,4},{1,7},{3,1},{5,3},{7,5},{8,14},{10,8},{12,... | collective-permute-start | bytes 786440 | tf_op jit(solution)/shard_map/ppermute | solution.py:121
  189.4 2.8 %collective-permute-start.6 = (bf16[128,1024]{1,0:T(8,128)(2,1)S(1)}, bf16[128,1024]{1,0:T(8,128)(2,1)S(1)}, u32[]{:S(2)}, u32[]{:S(2)}) collective-permute-start(bf16[128,1024]{1,0:T(8,128)(2,1)S(1)} %bitcast.73), channel_id=1, source_target_pairs={{0,2},{2,4},{4,6},{6,0},{1,3},{3,5},{5,7},{7,1},{8,10},{10,12},{12... | collective-permute-start | bytes 786440 | tf_op jit(solution)/shard_map/ppermute | solution.py:121
  192.1 2.5 %collective-permute-start.5 = (bf16[128,1024]{1,0:T(8,128)(2,1)S(1)}, bf16[128,1024]{1,0:T(8,128)(2,1)S(1)}, u32[]{:S(2)}, u32[]{:S(2)}) collective-permute-start(bf16[128,1024]{1,0:T(8,128)(2,1)S(1)} %bitcast.74), channel_id=1, source_target_pairs={{0,4},{2,6},{4,0},{6,2},{1,5},{3,7},{5,1},{7,3},{8,12},{10,14},{12... | collective-permute-start | bytes 786440 | tf_op jit(solution)/shard_map/ppermute | solution.py:121
  194.7 1.9 fusion.31
  196.5 0.7 slice_bitcast_fusion
  197.2 17.6 %collective-permute-done.8 = bf16[128,1024]{1,0:T(8,128)(2,1)S(1)} collective-permute-done((bf16[128,1024]{1,0:T(8,128)(2,1)S(1)}, bf16[128,1024]{1,0:T(8,128)(2,1)S(1)}, u32[]{:S(2)}, u32[]{:S(2)}) %collective-permute-start.8) | collective-permute-done | bytes 262176 | tf_op jit(solution)/shard_map/ppermute | solution.py:35
  214.8 0.0 collective-permute-done.7
  214.8 0.0 collective-permute-done.6
  214.8 0.0 collective-permute-done.5
  214.8 1.1 broadcast_in_dim.53
  215.9 3.5 %all-to-all-start.7 = ((bf16[4,128,1024]{2,1,0:T(8,128)(2,1)}), bf16[4,128,1024]{2,1,0:T(8,128)(2,1)S(1)}, u32[]{:S(2)}, u32[]{:S(2)}) async-start(bf16[4,128,1024]{2,1,0:T(8,128)(2,1)} %broadcast_in_dim.53), calls=%async_computation.7 | async-start | bytes 2097152 | tf_op jit(solution)/shard_map/all_to_all | solution.py:39
  219.7 0.1 constant_dynamic-slice_fusion
  219.7 0.3 broadcast_in_dim.51
  220.0 0.1 copy_dynamic-update-slice_fusion.1
  220.1 14.8 %all-to-all-done.7 = bf16[4,128,1024]{2,1,0:T(8,128)(2,1)S(1)} async-done(((bf16[4,128,1024]{2,1,0:T(8,128)(2,1)}), bf16[4,128,1024]{2,1,0:T(8,128)(2,1)S(1)}, u32[]{:S(2)}, u32[]{:S(2)}) %all-to-all-start.7) | async-done | bytes 1048608 | tf_op jit(solution)/shard_map/all_to_all | solution.py:39
  234.9 0.1 copy_dynamic-update-slice_fusion
  235.0 0.0 copy-start
  235.1 1.3 copy-done
  (21 shorter events, 0.3 us)
Async XLA Ops:
  0.6 46.8 %copy-start.3 = (bf16[384,1024]{1,0:T(8,128)(2,1)S(1)}, bf16[384,1024]{1,0:T(8,128)(2,1)}, u32[]{:S(2)}) copy-start(bf16[384,1024]{1,0:T(8,128)(2,1)} %param.6) | copy-start | bytes 2359300
  2.2 28.9 %all-to-all-start = ((bf16[8,16,1024]{2,1,0:T(8,128)(2,1)}), bf16[8,16,1024]{2,1,0:T(8,128)(2,1)S(1)}, u32[]{:S(2)}, u32[]{:S(2)}) async-start(bf16[8,16,1024]{2,1,0:T(8,128)(2,1)} %broadcast_in_dim.22), calls=%async_computation | async-start | bytes 524288 | tf_op jit(solution)/shard_map/all_to_all | solution.py:39
  14.8 21.7 %collective-permute-start.1 = (bf16[384,1024]{1,0:T(8,128)(2,1)}, bf16[384,1024]{1,0:T(8,128)(2,1)S(1)}, u32[]{:S(2)}, u32[]{:S(2)}) collective-permute-start(bf16[384,1024]{1,0:T(8,128)(2,1)} %param.6), channel_id=1, source_target_pairs={{0,8},{8,0},{1,9},{9,1},{2,10},{10,2},{3,11},{11,3},{4,12},{12,4},... | collective-permute-start | bytes 2359304 | tf_op jit(solution)/shard_map/ppermute | solution.py:35
  32.2 15.2 %all-to-all-start.1 = ((bf16[4,128,1024]{2,1,0:T(8,128)(2,1)}), bf16[4,128,1024]{2,1,0:T(8,128)(2,1)S(1)}, u32[]{:S(2)}, u32[]{:S(2)}) async-start(bf16[4,128,1024]{2,1,0:T(8,128)(2,1)} %broadcast_in_dim.48), calls=%async_computation.1 | async-start | bytes 2097152 | tf_op jit(solution)/shard_map/all_to_all | solution.py:39
  48.5 22.4 %copy-start.4 = (bf16[384,1024]{1,0:T(8,128)(2,1)S(1)}, bf16[384,1024]{1,0:T(8,128)(2,1)}, u32[]{:S(2)}) copy-start(bf16[384,1024]{1,0:T(8,128)(2,1)} %param.7) | copy-start | bytes 2359300
  62.7 21.5 %collective-permute-start.2 = (f16[192,512]{1,0:T(8,128)(2,1)S(1)}, f16[192,512]{1,0:T(8,128)(2,1)S(1)}, u32[]{:S(2)}, u32[]{:S(2)}) collective-permute-start(f16[192,512]{1,0:T(8,128)(2,1)S(1)} %multiply_convert_fusion.3), channel_id=1, source_target_pairs={{0,1},{1,0},{2,3},{3,2},{4,5},{5,4},{6,7},{7,6},{8,9},{9,8},{10,11... | collective-permute-start | bytes 589832 | tf_op jit(solution)/shard_map/ppermute | solution.py:35
  71.0 17.8 %collective-permute-start = (bf16[384,1024]{1,0:T(8,128)(2,1)S(1)}, bf16[384,1024]{1,0:T(8,128)(2,1)S(1)}, u32[]{:S(2)}, u32[]{:S(2)}) collective-permute-start(bf16[384,1024]{1,0:T(8,128)(2,1)S(1)} %copy-done.4), channel_id=1, source_target_pairs={{0,8},{8,0},{1,9},{9,1},{2,10},{10,2},{3,11},{11,3},{4,12},{12,4},... | collective-permute-start | bytes 2359304 | tf_op jit(solution)/shard_map/ppermute | solution.py:35
  85.3 13.0 %all-to-all-start.3 = ((bf16[4,192,512]{2,1,0:T(8,128)(2,1)}), bf16[4,192,512]{2,1,0:T(8,128)(2,1)S(1)}, u32[]{:S(2)}, u32[]{:S(2)}) async-start(bf16[4,192,512]{2,1,0:T(8,128)(2,1)} %broadcast_in_dim.49), calls=%async_computation.3 | async-start | bytes 1572864 | tf_op jit(solution)/shard_map/all_to_all | solution.py:39
  100.5 14.4 %all-to-all-start.4 = ((f16[4,256,512]{2,1,0:T(8,128)(2,1)}), f16[4,256,512]{2,1,0:T(8,128)(2,1)S(1)}, u32[]{:S(2)}, u32[]{:S(2)}) async-start(f16[4,256,512]{2,1,0:T(8,128)(2,1)} %bitcast.7), calls=%async_computation.4 | async-start | bytes 2097152 | tf_op jit(solution)/shard_map/all_to_all | solution.py:39
  104.0 32.5 %copy-start.1 = (f32[1,16,1024]{2,1,0:T(8,128)S(1)}, f32[1,16,1024]{2,1,0:T(8,128)}, u32[]{:S(2)}) copy-start(f32[1,16,1024]{2,1,0:T(8,128)} %param.11) | copy-start | bytes 196612
  104.0 32.5 %copy-start.2 = (f32[1,16,1024]{2,1,0:T(8,128)S(1)}, f32[1,16,1024]{2,1,0:T(8,128)}, u32[]{:S(2)}) copy-start(f32[1,16,1024]{2,1,0:T(8,128)} %param.10) | copy-start | bytes 196612
  104.1 64.8 %collective-permute-start.4 = (bf16[512,1024]{1,0:T(8,128)(2,1)S(1)}, bf16[512,1024]{1,0:T(8,128)(2,1)}, u32[]{:S(2)}, u32[]{:S(2)}) collective-permute-start(bf16[512,1024]{1,0:T(8,128)(2,1)S(1)} %bitcast.63), channel_id=1, source_target_pairs={{0,8},{8,0},{1,9},{9,1},{2,10},{10,2},{3,11},{11,3},{4,12},{12,4},... | collective-permute-start | bytes 3145736 | tf_op jit(solution)/shard_map/ppermute | solution.py:35
  116.0 34.0 %all-to-all-start.5 = ((f16[16,16,512]{2,1,0:T(8,128)(2,1)}), f16[16,16,512]{2,1,0:T(8,128)(2,1)S(1)}, u32[]{:S(2)}, u32[]{:S(2)}) async-start(f16[16,16,512]{2,1,0:T(8,128)(2,1)} %multiply_convert_fusion.2), calls=%async_computation.5 | async-start | bytes 524288 | tf_op jit(solution)/shard_map/all_to_all | solution.py:39
  150.2 14.5 %collective-permute-start.3 = (bf16[16,1024]{1,0:T(8,128)(2,1)S(1)}, bf16[16,1024]{1,0:T(8,128)(2,1)S(1)}, u32[]{:S(2)}, u32[]{:S(2)}) collective-permute-start(bf16[16,1024]{1,0:T(8,128)(2,1)S(1)} %get-tuple-element.14), channel_id=1, source_target_pairs={{0,1},{1,0},{2,3},{3,2},{4,5},{5,4},{6,7},{7,6},{8,9},{9,8},{10,11... | collective-permute-start | bytes 98312 | tf_op jit(solution)/shard_map/ppermute | solution.py:35
  165.5 11.4 %all-to-all-start.6 = ((bf16[4,32,1024]{2,1,0:T(8,128)(2,1)}), bf16[4,32,1024]{2,1,0:T(8,128)(2,1)S(1)}, u32[]{:S(2)}, u32[]{:S(2)}) async-start(bf16[4,32,1024]{2,1,0:T(8,128)(2,1)} %broadcast_in_dim.50), calls=%async_computation.6 | async-start | bytes 524288 | tf_op jit(solution)/shard_map/all_to_all | solution.py:39
  179.6 35.2 %collective-permute-start.8 = (bf16[128,1024]{1,0:T(8,128)(2,1)S(1)}, bf16[128,1024]{1,0:T(8,128)(2,1)S(1)}, u32[]{:S(2)}, u32[]{:S(2)}) collective-permute-start(bf16[128,1024]{1,0:T(8,128)(2,1)S(1)} %bitcast.71), channel_id=1, source_target_pairs={{0,1},{1,0},{2,3},{3,2},{4,5},{5,4},{6,7},{7,6},{8,9},{9,8},{10,11... | collective-permute-start | bytes 786440 | tf_op jit(solution)/shard_map/ppermute | solution.py:35
  186.3 28.5 %collective-permute-start.7 = (bf16[128,1024]{1,0:T(8,128)(2,1)S(1)}, bf16[128,1024]{1,0:T(8,128)(2,1)S(1)}, u32[]{:S(2)}, u32[]{:S(2)}) collective-permute-start(bf16[128,1024]{1,0:T(8,128)(2,1)S(1)} %bitcast.72), channel_id=1, source_target_pairs={{0,6},{2,0},{4,2},{6,4},{1,7},{3,1},{5,3},{7,5},{8,14},{10,8},{12,... | collective-permute-start | bytes 786440 | tf_op jit(solution)/shard_map/ppermute | solution.py:121
  189.4 25.4 %collective-permute-start.6 = (bf16[128,1024]{1,0:T(8,128)(2,1)S(1)}, bf16[128,1024]{1,0:T(8,128)(2,1)S(1)}, u32[]{:S(2)}, u32[]{:S(2)}) collective-permute-start(bf16[128,1024]{1,0:T(8,128)(2,1)S(1)} %bitcast.73), channel_id=1, source_target_pairs={{0,2},{2,4},{4,6},{6,0},{1,3},{3,5},{5,7},{7,1},{8,10},{10,12},{12... | collective-permute-start | bytes 786440 | tf_op jit(solution)/shard_map/ppermute | solution.py:121
  192.1 22.7 %collective-permute-start.5 = (bf16[128,1024]{1,0:T(8,128)(2,1)S(1)}, bf16[128,1024]{1,0:T(8,128)(2,1)S(1)}, u32[]{:S(2)}, u32[]{:S(2)}) collective-permute-start(bf16[128,1024]{1,0:T(8,128)(2,1)S(1)} %bitcast.74), channel_id=1, source_target_pairs={{0,4},{2,6},{4,0},{6,2},{1,5},{3,7},{5,1},{7,3},{8,12},{10,14},{12... | collective-permute-start | bytes 786440 | tf_op jit(solution)/shard_map/ppermute | solution.py:121
  215.9 19.0 %all-to-all-start.7 = ((bf16[4,128,1024]{2,1,0:T(8,128)(2,1)}), bf16[4,128,1024]{2,1,0:T(8,128)(2,1)S(1)}, u32[]{:S(2)}, u32[]{:S(2)}) async-start(bf16[4,128,1024]{2,1,0:T(8,128)(2,1)} %broadcast_in_dim.53), calls=%async_computation.7 | async-start | bytes 2097152 | tf_op jit(solution)/shard_map/all_to_all | solution.py:39
  235.0 1.3 copy-start

commit v4 on v3

--- a/solution.py
+++ b/solution.py
@@ -22,12 +22,15 @@
 SWAP = [(0, 1), (1, 0)]
 
 
+root_scale = 32.0
+
+
 def encode(value):
-    return (value * lax.rsqrt(jnp.abs(value) + 1e-30)).astype(f16)
+    return (value * (root_scale * lax.rsqrt(jnp.abs(value) + 1e-30))).astype(f16)
 
 
 def decode(coded):
-    root = coded.astype(f32)
+    root = coded.astype(f32) * (1.0 / root_scale)
     return root * jnp.abs(root)
 
 

time: 237 us -> 238 us (level)
  no operation moved by 1% of the time
where the time goes in v4:
time: 238 us; the launch traced here: 237 us
  waiting for transfers between devices  113 us (47%)
  starting transfers between devices  86.3 us (36%)
  blocking collectives  13.9 us (6%)
  matrix products  9.31 us (4%)
  local copies, waits for them, and re-layouts  8.15 us (3%)
  other arithmetic  4.97 us (2%)
    all_to_all x7, waiting for transfers between devices, exchange(): return lax.all_to_all(value, axis, 0, 0)  76.2 us
    all_to_all x7, starting transfers between devices, exchange(): return lax.all_to_all(value, axis, 0, 0)  50.6 us
    ppermute x6, waiting for transfers between devices, swap(): return lax.ppermute(value, axis, SWAP)  36.8 us
    ppermute x6, starting transfers between devices, swap(): return lax.ppermute(value, axis, SWAP)  27.3 us
    all_to_all x1, blocking collectives, exchange(): return lax.all_to_all(value, axis, 0, 0)  13.9 us
    ppermute x3, starting transfers between devices, on_device(): lax.ppermute(block_forward, 'y', [(i, (i + d) % Y) for i in range(Y)])  8.37 us
    broadcast_in_dim x5, local copies, waits for them, and re-layouts, gather(): return exchange(jnp.broadcast_to(value[None], (count, *value.shape)), axis)  5.43 us
  transfers between devices with their start and end apart: 16, of which 10 were waited for; matrix products, arithmetic and copies ran while one was open for 5% of the time, Pallas kernels for 0%

profile of v4, /device:TPU:32, one launch (start us, length us, event | category | flops | bytes accessed | tf_op | source)
XLA Modules:
  0.0 236.7 jit_solution(4595456196452724489)
XLA Ops:
  0.6 0.0 copy-start.3
  0.6 1.6 broadcast_in_dim.22
  2.2 12.6 %all-to-all-start = ((bf16[8,16,1024]{2,1,0:T(8,128)(2,1)}), bf16[8,16,1024]{2,1,0:T(8,128)(2,1)S(1)}, u32[]{:S(2)}, u32[]{:S(2)}) async-start(bf16[8,16,1024]{2,1,0:T(8,128)(2,1)} %broadcast_in_dim.22), calls=%async_computation | async-start | bytes 524288 | tf_op jit(solution)/shard_map/all_to_all | solution.py:42
  14.8 1.9 collective-permute-start.1
  16.8 14.4 %all-to-all-done = bf16[8,16,1024]{2,1,0:T(8,128)(2,1)S(1)} async-done(((bf16[8,16,1024]{2,1,0:T(8,128)(2,1)}), bf16[8,16,1024]{2,1,0:T(8,128)(2,1)S(1)}, u32[]{:S(2)}, u32[]{:S(2)}) %all-to-all-start) | async-done | bytes 262176 | tf_op jit(solution)/shard_map/all_to_all | solution.py:42
  31.1 1.1 broadcast_in_dim.48
  32.2 4.3 %all-to-all-start.1 = ((bf16[4,128,1024]{2,1,0:T(8,128)(2,1)}), bf16[4,128,1024]{2,1,0:T(8,128)(2,1)S(1)}, u32[]{:S(2)}, u32[]{:S(2)}) async-start(bf16[4,128,1024]{2,1,0:T(8,128)(2,1)} %broadcast_in_dim.48), calls=%async_computation.1 | async-start | bytes 2097152 | tf_op jit(solution)/shard_map/all_to_all | solution.py:42
  36.5 0.0 collective-permute-done.1
  36.5 10.9 %all-to-all-done.1 = bf16[4,128,1024]{2,1,0:T(8,128)(2,1)S(1)} async-done(((bf16[4,128,1024]{2,1,0:T(8,128)(2,1)}), bf16[4,128,1024]{2,1,0:T(8,128)(2,1)S(1)}, u32[]{:S(2)}, u32[]{:S(2)}) %all-to-all-start.1) | async-done | bytes 1048608 | tf_op jit(solution)/shard_map/all_to_all | solution.py:42
  47.4 1.2 multiply_convert_fusion.1
  48.6 0.0 copy-start.4
  48.6 13.9 %all_to_all.40 = f16[4,192,512]{2,1,0:T(8,128)(2,1)S(1)} all-to-all(f16[4,192,512]{2,1,0:T(8,128)(2,1)S(1)} %bitcast.78), channel_id=1, replica_groups=mesh['x'=4,'zl'=8,'c'=2,'y'=4,'zh'=2] {'y'}, dimensions={0} | all-to-all | bytes 1572864 | tf_op jit(solution)/shard_map/all_to_all | solution.py:42
  62.5 0.3 fusion.13
  62.7 0.1 multiply_convert_fusion.3
  62.8 8.2 %collective-permute-start.2 = (f16[192,512]{1,0:T(8,128)(2,1)S(1)}, f16[192,512]{1,0:T(8,128)(2,1)S(1)}, u32[]{:S(2)}, u32[]{:S(2)}) collective-permute-start(f16[192,512]{1,0:T(8,128)(2,1)S(1)} %multiply_convert_fusion.3), channel_id=1, source_target_pairs={{0,1},{1,0},{2,3},{3,2},{4,5},{5,4},{6,7},{7,6},{8,9},{9,8},{10,11... | collective-permute-start | bytes 589832 | tf_op jit(solution)/shard_map/ppermute | solution.py:38
  71.1 0.0 copy-done.4
  71.1 1.9 collective-permute-start
  73.0 11.4 %collective-permute-done.2 = f16[192,512]{1,0:T(8,128)(2,1)S(1)} collective-permute-done((f16[192,512]{1,0:T(8,128)(2,1)S(1)}, f16[192,512]{1,0:T(8,128)(2,1)S(1)}, u32[]{:S(2)}, u32[]{:S(2)}) %collective-permute-start.2) | collective-permute-done | bytes 196640 | tf_op jit(solution)/shard_map/ppermute | solution.py:38
  84.4 0.1 fusion.26
  84.4 0.9 broadcast_in_dim.49
  85.4 3.5 %all-to-all-start.3 = ((bf16[4,192,512]{2,1,0:T(8,128)(2,1)}), bf16[4,192,512]{2,1,0:T(8,128)(2,1)S(1)}, u32[]{:S(2)}, u32[]{:S(2)}) async-start(bf16[4,192,512]{2,1,0:T(8,128)(2,1)} %broadcast_in_dim.49), calls=%async_computation.3 | async-start | bytes 1572864 | tf_op jit(solution)/shard_map/all_to_all | solution.py:42
  88.9 0.0 collective-permute-done
  88.9 9.4 %all-to-all-done.3 = bf16[4,192,512]{2,1,0:T(8,128)(2,1)S(1)} async-done(((bf16[4,192,512]{2,1,0:T(8,128)(2,1)}), bf16[4,192,512]{2,1,0:T(8,128)(2,1)S(1)}, u32[]{:S(2)}, u32[]{:S(2)}) %all-to-all-start.3) | async-done | bytes 786464 | tf_op jit(solution)/shard_map/all_to_all | solution.py:42
  98.3 2.3 multiply_convert_fusion
  100.7 3.5 %all-to-all-start.4 = ((f16[4,256,512]{2,1,0:T(8,128)(2,1)}), f16[4,256,512]{2,1,0:T(8,128)(2,1)S(1)}, u32[]{:S(2)}, u32[]{:S(2)}) async-start(f16[4,256,512]{2,1,0:T(8,128)(2,1)} %bitcast.7), calls=%async_computation.4 | async-start | bytes 2097152 | tf_op jit(solution)/shard_map/all_to_all | solution.py:42
  104.2 0.0 copy-start.1
  104.2 0.0 copy-start.2
  104.3 1.9 collective-permute-start.4
  106.2 8.8 %all-to-all-done.4 = f16[4,256,512]{2,1,0:T(8,128)(2,1)S(1)} async-done(((f16[4,256,512]{2,1,0:T(8,128)(2,1)}), f16[4,256,512]{2,1,0:T(8,128)(2,1)S(1)}, u32[]{:S(2)}, u32[]{:S(2)}) %all-to-all-start.4) | async-done | bytes 1048608 | tf_op jit(solution)/shard_map/all_to_all | solution.py:42
  115.1 0.4 fusion.9
  115.4 0.8 multiply_convert_fusion.2
  116.2 19.8 %all-to-all-start.5 = ((f16[16,16,512]{2,1,0:T(8,128)(2,1)}), f16[16,16,512]{2,1,0:T(8,128)(2,1)S(1)}, u32[]{:S(2)}, u32[]{:S(2)}) async-start(f16[16,16,512]{2,1,0:T(8,128)(2,1)} %multiply_convert_fusion.2), calls=%async_computation.5 | async-start | bytes 524288 | tf_op jit(solution)/shard_map/all_to_all | solution.py:42
  136.0 0.8 fusion.4
  136.8 1.3 fusion.27
  138.1 12.2 %all-to-all-done.5 = f16[16,16,512]{2,1,0:T(8,128)(2,1)S(1)} async-done(((f16[16,16,512]{2,1,0:T(8,128)(2,1)}), f16[16,16,512]{2,1,0:T(8,128)(2,1)S(1)}, u32[]{:S(2)}, u32[]{:S(2)}) %all-to-all-start.5) | async-done | bytes 262176 | tf_op jit(solution)/shard_map/all_to_all | solution.py:42
  150.3 0.1 abs_multiply_fusion.2
  150.5 0.1 divide_convert_fusion
  150.5 6.7 %collective-permute-start.3 = (bf16[16,1024]{1,0:T(8,128)(2,1)S(1)}, bf16[16,1024]{1,0:T(8,128)(2,1)S(1)}, u32[]{:S(2)}, u32[]{:S(2)}) collective-permute-start(bf16[16,1024]{1,0:T(8,128)(2,1)S(1)} %get-tuple-element.14), channel_id=1, source_target_pairs={{0,1},{1,0},{2,3},{3,2},{4,5},{5,4},{6,7},{7,6},{8,9},{9,8},{10,11... | collective-permute-start | bytes 98312 | tf_op jit(solution)/shard_map/ppermute | solution.py:38
  157.2 7.8 %collective-permute-done.3 = bf16[16,1024]{1,0:T(8,128)(2,1)S(1)} collective-permute-done((bf16[16,1024]{1,0:T(8,128)(2,1)S(1)}, bf16[16,1024]{1,0:T(8,128)(2,1)S(1)}, u32[]{:S(2)}, u32[]{:S(2)}) %collective-permute-start.3) | collective-permute-done | bytes 32800 | tf_op jit(solution)/shard_map/ppermute | solution.py:38
  165.1 0.7 broadcast_in_dim.50
  165.8 3.4 %all-to-all-start.6 = ((bf16[4,32,1024]{2,1,0:T(8,128)(2,1)}), bf16[4,32,1024]{2,1,0:T(8,128)(2,1)S(1)}, u32[]{:S(2)}, u32[]{:S(2)}) async-start(bf16[4,32,1024]{2,1,0:T(8,128)(2,1)} %broadcast_in_dim.50), calls=%async_computation.6 | async-start | bytes 524288 | tf_op jit(solution)/shard_map/all_to_all | solution.py:42
  169.2 0.0 collective-permute-done.4
  169.2 2.3 broadcast_select_fusion.1
  171.6 5.6 %all-to-all-done.6 = bf16[4,32,1024]{2,1,0:T(8,128)(2,1)S(1)} async-done(((bf16[4,32,1024]{2,1,0:T(8,128)(2,1)}), bf16[4,32,1024]{2,1,0:T(8,128)(2,1)S(1)}, u32[]{:S(2)}, u32[]{:S(2)}) %all-to-all-start.6) | async-done | bytes 262176 | tf_op jit(solution)/shard_map/all_to_all | solution.py:42
  177.3 2.6 %fusion.54 = (bf16[8,16,1024]{2,1,0:T(8,128)(2,1)S(1)}, f32[8,16,1024]{2,1,0:T(8,128)}) fusion(f32[8,16,1024]{2,1,0:T(8,128)} %param.9, bf16[8,16,1024]{2,1,0:T(8,128)(2,1)S(1)} %bitcast.79, bf16[512,1024]{1,0:T(8,128)(2,1)} %get-tuple-element.18, bf16[512,1024]{1,0:T(8,128)(2,1)S(1)} %get-tuple-element.17), kind=kOutput, calls=%fused_computation.97 | convolution fusion | flops 273022976 | bytes 3670016 | tf_op jit(solution)/shard_map/dot_general | solution.py:117
  179.9 6.7 %collective-permute-start.8 = (bf16[128,1024]{1,0:T(8,128)(2,1)S(1)}, bf16[128,1024]{1,0:T(8,128)(2,1)S(1)}, u32[]{:S(2)}, u32[]{:S(2)}) collective-permute-start(bf16[128,1024]{1,0:T(8,128)(2,1)S(1)} %bitcast.71), channel_id=1, source_target_pairs={{0,1},{1,0},{2,3},{3,2},{4,5},{5,4},{6,7},{7,6},{8,9},{9,8},{10,11... | collective-permute-start | bytes 786440 | tf_op jit(solution)/shard_map/ppermute | solution.py:38
  186.6 3.1 %collective-permute-start.7 = (bf16[128,1024]{1,0:T(8,128)(2,1)S(1)}, bf16[128,1024]{1,0:T(8,128)(2,1)S(1)}, u32[]{:S(2)}, u32[]{:S(2)}) collective-permute-start(bf16[128,1024]{1,0:T(8,128)(2,1)S(1)} %bitcast.72), channel_id=1, source_target_pairs={{0,6},{2,0},{4,2},{6,4},{1,7},{3,1},{5,3},{7,5},{8,14},{10,8},{12,... | collective-permute-start | bytes 786440 | tf_op jit(solution)/shard_map/ppermute | solution.py:124
  189.6 2.8 %collective-permute-start.6 = (bf16[128,1024]{1,0:T(8,128)(2,1)S(1)}, bf16[128,1024]{1,0:T(8,128)(2,1)S(1)}, u32[]{:S(2)}, u32[]{:S(2)}) collective-permute-start(bf16[128,1024]{1,0:T(8,128)(2,1)S(1)} %bitcast.73), channel_id=1, source_target_pairs={{0,2},{2,4},{4,6},{6,0},{1,3},{3,5},{5,7},{7,1},{8,10},{10,12},{12... | collective-permute-start | bytes 786440 | tf_op jit(solution)/shard_map/ppermute | solution.py:124
  192.4 2.5 %collective-permute-start.5 = (bf16[128,1024]{1,0:T(8,128)(2,1)S(1)}, bf16[128,1024]{1,0:T(8,128)(2,1)S(1)}, u32[]{:S(2)}, u32[]{:S(2)}) collective-permute-start(bf16[128,1024]{1,0:T(8,128)(2,1)S(1)} %bitcast.74), channel_id=1, source_target_pairs={{0,4},{2,6},{4,0},{6,2},{1,5},{3,7},{5,1},{7,3},{8,12},{10,14},{12... | collective-permute-start | bytes 786440 | tf_op jit(solution)/shard_map/ppermute | solution.py:124
  195.0 1.9 fusion.31
  196.8 0.7 slice_bitcast_fusion
  197.5 17.6 %collective-permute-done.8 = bf16[128,1024]{1,0:T(8,128)(2,1)S(1)} collective-permute-done((bf16[128,1024]{1,0:T(8,128)(2,1)S(1)}, bf16[128,1024]{1,0:T(8,128)(2,1)S(1)}, u32[]{:S(2)}, u32[]{:S(2)}) %collective-permute-start.8) | collective-permute-done | bytes 262176 | tf_op jit(solution)/shard_map/ppermute | solution.py:38
  215.1 0.0 collective-permute-done.7
  215.1 0.0 collective-permute-done.6
  215.1 0.0 collective-permute-done.5
  215.1 1.1 broadcast_in_dim.53
  216.2 3.5 %all-to-all-start.7 = ((bf16[4,128,1024]{2,1,0:T(8,128)(2,1)}), bf16[4,128,1024]{2,1,0:T(8,128)(2,1)S(1)}, u32[]{:S(2)}, u32[]{:S(2)}) async-start(bf16[4,128,1024]{2,1,0:T(8,128)(2,1)} %broadcast_in_dim.53), calls=%async_computation.7 | async-start | bytes 2097152 | tf_op jit(solution)/shard_map/all_to_all | solution.py:42
  220.0 0.1 constant_dynamic-slice_fusion
  220.0 0.3 broadcast_in_dim.51
  220.3 0.1 copy_dynamic-update-slice_fusion.1
  220.4 14.8 %all-to-all-done.7 = bf16[4,128,1024]{2,1,0:T(8,128)(2,1)S(1)} async-done(((bf16[4,128,1024]{2,1,0:T(8,128)(2,1)}), bf16[4,128,1024]{2,1,0:T(8,128)(2,1)S(1)}, u32[]{:S(2)}, u32[]{:S(2)}) %all-to-all-start.7) | async-done | bytes 1048608 | tf_op jit(solution)/shard_map/all_to_all | solution.py:42
  235.2 0.1 copy_dynamic-update-slice_fusion
  235.4 0.0 copy-start
  235.4 1.3 copy-done
  (21 shorter events, 0.3 us)
Async XLA Ops:
  0.6 46.8 %copy-start.3 = (bf16[384,1024]{1,0:T(8,128)(2,1)S(1)}, bf16[384,1024]{1,0:T(8,128)(2,1)}, u32[]{:S(2)}) copy-start(bf16[384,1024]{1,0:T(8,128)(2,1)} %param.6) | copy-start | bytes 2359300
  2.2 28.9 %all-to-all-start = ((bf16[8,16,1024]{2,1,0:T(8,128)(2,1)}), bf16[8,16,1024]{2,1,0:T(8,128)(2,1)S(1)}, u32[]{:S(2)}, u32[]{:S(2)}) async-start(bf16[8,16,1024]{2,1,0:T(8,128)(2,1)} %broadcast_in_dim.22), calls=%async_computation | async-start | bytes 524288 | tf_op jit(solution)/shard_map/all_to_all | solution.py:42
  14.8 21.7 %collective-permute-start.1 = (bf16[384,1024]{1,0:T(8,128)(2,1)}, bf16[384,1024]{1,0:T(8,128)(2,1)S(1)}, u32[]{:S(2)}, u32[]{:S(2)}) collective-permute-start(bf16[384,1024]{1,0:T(8,128)(2,1)} %param.6), channel_id=1, source_target_pairs={{0,8},{8,0},{1,9},{9,1},{2,10},{10,2},{3,11},{11,3},{4,12},{12,4},... | collective-permute-start | bytes 2359304 | tf_op jit(solution)/shard_map/ppermute | solution.py:38
  32.2 15.2 %all-to-all-start.1 = ((bf16[4,128,1024]{2,1,0:T(8,128)(2,1)}), bf16[4,128,1024]{2,1,0:T(8,128)(2,1)S(1)}, u32[]{:S(2)}, u32[]{:S(2)}) async-start(bf16[4,128,1024]{2,1,0:T(8,128)(2,1)} %broadcast_in_dim.48), calls=%async_computation.1 | async-start | bytes 2097152 | tf_op jit(solution)/shard_map/all_to_all | solution.py:42
  48.6 22.5 %copy-start.4 = (bf16[384,1024]{1,0:T(8,128)(2,1)S(1)}, bf16[384,1024]{1,0:T(8,128)(2,1)}, u32[]{:S(2)}) copy-start(bf16[384,1024]{1,0:T(8,128)(2,1)} %param.7) | copy-start | bytes 2359300
  62.8 21.5 %collective-permute-start.2 = (f16[192,512]{1,0:T(8,128)(2,1)S(1)}, f16[192,512]{1,0:T(8,128)(2,1)S(1)}, u32[]{:S(2)}, u32[]{:S(2)}) collective-permute-start(f16[192,512]{1,0:T(8,128)(2,1)S(1)} %multiply_convert_fusion.3), channel_id=1, source_target_pairs={{0,1},{1,0},{2,3},{3,2},{4,5},{5,4},{6,7},{7,6},{8,9},{9,8},{10,11... | collective-permute-start | bytes 589832 | tf_op jit(solution)/shard_map/ppermute | solution.py:38
  71.1 17.8 %collective-permute-start = (bf16[384,1024]{1,0:T(8,128)(2,1)S(1)}, bf16[384,1024]{1,0:T(8,128)(2,1)S(1)}, u32[]{:S(2)}, u32[]{:S(2)}) collective-permute-start(bf16[384,1024]{1,0:T(8,128)(2,1)S(1)} %copy-done.4), channel_id=1, source_target_pairs={{0,8},{8,0},{1,9},{9,1},{2,10},{10,2},{3,11},{11,3},{4,12},{12,4},... | collective-permute-start | bytes 2359304 | tf_op jit(solution)/shard_map/ppermute | solution.py:38
  85.4 13.0 %all-to-all-start.3 = ((bf16[4,192,512]{2,1,0:T(8,128)(2,1)}), bf16[4,192,512]{2,1,0:T(8,128)(2,1)S(1)}, u32[]{:S(2)}, u32[]{:S(2)}) async-start(bf16[4,192,512]{2,1,0:T(8,128)(2,1)} %broadcast_in_dim.49), calls=%async_computation.3 | async-start | bytes 1572864 | tf_op jit(solution)/shard_map/all_to_all | solution.py:42
  100.7 14.4 %all-to-all-start.4 = ((f16[4,256,512]{2,1,0:T(8,128)(2,1)}), f16[4,256,512]{2,1,0:T(8,128)(2,1)S(1)}, u32[]{:S(2)}, u32[]{:S(2)}) async-start(f16[4,256,512]{2,1,0:T(8,128)(2,1)} %bitcast.7), calls=%async_computation.4 | async-start | bytes 2097152 | tf_op jit(solution)/shard_map/all_to_all | solution.py:42
  104.2 32.6 %copy-start.1 = (f32[1,16,1024]{2,1,0:T(8,128)S(1)}, f32[1,16,1024]{2,1,0:T(8,128)}, u32[]{:S(2)}) copy-start(f32[1,16,1024]{2,1,0:T(8,128)} %param.11) | copy-start | bytes 196612
  104.2 32.6 %copy-start.2 = (f32[1,16,1024]{2,1,0:T(8,128)S(1)}, f32[1,16,1024]{2,1,0:T(8,128)}, u32[]{:S(2)}) copy-start(f32[1,16,1024]{2,1,0:T(8,128)} %param.10) | copy-start | bytes 196612
  104.3 64.9 %collective-permute-start.4 = (bf16[512,1024]{1,0:T(8,128)(2,1)S(1)}, bf16[512,1024]{1,0:T(8,128)(2,1)}, u32[]{:S(2)}, u32[]{:S(2)}) collective-permute-start(bf16[512,1024]{1,0:T(8,128)(2,1)S(1)} %bitcast.63), channel_id=1, source_target_pairs={{0,8},{8,0},{1,9},{9,1},{2,10},{10,2},{3,11},{11,3},{4,12},{12,4},... | collective-permute-start | bytes 3145736 | tf_op jit(solution)/shard_map/ppermute | solution.py:38
  116.2 34.1 %all-to-all-start.5 = ((f16[16,16,512]{2,1,0:T(8,128)(2,1)}), f16[16,16,512]{2,1,0:T(8,128)(2,1)S(1)}, u32[]{:S(2)}, u32[]{:S(2)}) async-start(f16[16,16,512]{2,1,0:T(8,128)(2,1)} %multiply_convert_fusion.2), calls=%async_computation.5 | async-start | bytes 524288 | tf_op jit(solution)/shard_map/all_to_all | solution.py:42
  150.5 14.5 %collective-permute-start.3 = (bf16[16,1024]{1,0:T(8,128)(2,1)S(1)}, bf16[16,1024]{1,0:T(8,128)(2,1)S(1)}, u32[]{:S(2)}, u32[]{:S(2)}) collective-permute-start(bf16[16,1024]{1,0:T(8,128)(2,1)S(1)} %get-tuple-element.14), channel_id=1, source_target_pairs={{0,1},{1,0},{2,3},{3,2},{4,5},{5,4},{6,7},{7,6},{8,9},{9,8},{10,11... | collective-permute-start | bytes 98312 | tf_op jit(solution)/shard_map/ppermute | solution.py:38
  165.8 11.4 %all-to-all-start.6 = ((bf16[4,32,1024]{2,1,0:T(8,128)(2,1)}), bf16[4,32,1024]{2,1,0:T(8,128)(2,1)S(1)}, u32[]{:S(2)}, u32[]{:S(2)}) async-start(bf16[4,32,1024]{2,1,0:T(8,128)(2,1)} %broadcast_in_dim.50), calls=%async_computation.6 | async-start | bytes 524288 | tf_op jit(solution)/shard_map/all_to_all | solution.py:42
  179.9 35.2 %collective-permute-start.8 = (bf16[128,1024]{1,0:T(8,128)(2,1)S(1)}, bf16[128,1024]{1,0:T(8,128)(2,1)S(1)}, u32[]{:S(2)}, u32[]{:S(2)}) collective-permute-start(bf16[128,1024]{1,0:T(8,128)(2,1)S(1)} %bitcast.71), channel_id=1, source_target_pairs={{0,1},{1,0},{2,3},{3,2},{4,5},{5,4},{6,7},{7,6},{8,9},{9,8},{10,11... | collective-permute-start | bytes 786440 | tf_op jit(solution)/shard_map/ppermute | solution.py:38
  186.6 28.5 %collective-permute-start.7 = (bf16[128,1024]{1,0:T(8,128)(2,1)S(1)}, bf16[128,1024]{1,0:T(8,128)(2,1)S(1)}, u32[]{:S(2)}, u32[]{:S(2)}) collective-permute-start(bf16[128,1024]{1,0:T(8,128)(2,1)S(1)} %bitcast.72), channel_id=1, source_target_pairs={{0,6},{2,0},{4,2},{6,4},{1,7},{3,1},{5,3},{7,5},{8,14},{10,8},{12,... | collective-permute-start | bytes 786440 | tf_op jit(solution)/shard_map/ppermute | solution.py:124
  189.6 25.5 %collective-permute-start.6 = (bf16[128,1024]{1,0:T(8,128)(2,1)S(1)}, bf16[128,1024]{1,0:T(8,128)(2,1)S(1)}, u32[]{:S(2)}, u32[]{:S(2)}) collective-permute-start(bf16[128,1024]{1,0:T(8,128)(2,1)S(1)} %bitcast.73), channel_id=1, source_target_pairs={{0,2},{2,4},{4,6},{6,0},{1,3},{3,5},{5,7},{7,1},{8,10},{10,12},{12... | collective-permute-start | bytes 786440 | tf_op jit(solution)/shard_map/ppermute | solution.py:124
  192.4 22.7 %collective-permute-start.5 = (bf16[128,1024]{1,0:T(8,128)(2,1)S(1)}, bf16[128,1024]{1,0:T(8,128)(2,1)S(1)}, u32[]{:S(2)}, u32[]{:S(2)}) collective-permute-start(bf16[128,1024]{1,0:T(8,128)(2,1)S(1)} %bitcast.74), channel_id=1, source_target_pairs={{0,4},{2,6},{4,0},{6,2},{1,5},{3,7},{5,1},{7,3},{8,12},{10,14},{12... | collective-permute-start | bytes 786440 | tf_op jit(solution)/shard_map/ppermute | solution.py:124
  216.2 19.0 %all-to-all-start.7 = ((bf16[4,128,1024]{2,1,0:T(8,128)(2,1)}), bf16[4,128,1024]{2,1,0:T(8,128)(2,1)S(1)}, u32[]{:S(2)}, u32[]{:S(2)}) async-start(bf16[4,128,1024]{2,1,0:T(8,128)(2,1)} %broadcast_in_dim.53), calls=%async_computation.7 | async-start | bytes 2097152 | tf_op jit(solution)/shard_map/all_to_all | solution.py:42
  235.4 1.3 copy-start

commit v5 on v4

--- a/solution.py
+++ b/solution.py
@@ -110,10 +110,8 @@
 
     rows_low, rows_high = ordered(rows, rows_other, core)
     rows_all = jnp.concatenate([rows_low, rows_high], 0)
-    both = jnp.concatenate([update, swap(update, "zh")], 0)
-    updates = gather(both, "y", Y).reshape(Y, ZH, cols, rank)
-    low, up = ordered(updates[:, 0], updates[:, 1], high)
-    updates = jnp.stack([low, up], 1).reshape(Y * ZH * cols, rank)
+    both = jnp.concatenate(ordered(update, swap(update, "zh"), high), 0)
+    updates = gather(both, "y", Y).reshape(Y * ZH * cols, rank)
     delta = jnp.dot(updates, rows_all, preferred_element_type=f32)
     new_master = master - learn_rate * delta.reshape(master.shape)
     block_forward = new_master.astype(bf16).reshape(Y * ZH * cols, feats)

time: 238 us -> 238 us (level)
  transfers between devices with their start and end apart: 16 -> 16, of which waited for: 10 -> 10; matrix products, arithmetic and copies ran while one was open for 5% -> 4% of each run, Pallas kernels for 0% -> 0%
where the time goes in v5:
time: 238 us; the launch traced here: 237 us
  waiting for transfers between devices  113 us (47%)
  starting transfers between devices  87.1 us (37%)
  blocking collectives  13.9 us (6%)
  matrix products  9.38 us (4%)
  local copies, waits for them, and re-layouts  8.15 us (3%)
  other arithmetic  4.93 us (2%)
    all_to_all x7, waiting for transfers between devices, exchange(): return lax.all_to_all(value, axis, 0, 0)  76.1 us
    all_to_all x7, starting transfers between devices, exchange(): return lax.all_to_all(value, axis, 0, 0)  51.3 us
    ppermute x6, waiting for transfers between devices, swap(): return lax.ppermute(value, axis, SWAP)  36.8 us
    ppermute x6, starting transfers between devices, swap(): return lax.ppermute(value, axis, SWAP)  27.4 us
    all_to_all x1, blocking collectives, exchange(): return lax.all_to_all(value, axis, 0, 0)  13.9 us
    ppermute x3, starting transfers between devices, on_device(): lax.ppermute(block_forward, 'y', [(i, (i + d) % Y) for i in range(Y)])  8.37 us
    broadcast_in_dim x5, local copies, waits for them, and re-layouts, gather(): return exchange(jnp.broadcast_to(value[None], (count, *value.shape)), axis)  5.43 us
  transfers between devices with their start and end apart: 16, of which 10 were waited for; matrix products, arithmetic and copies ran while one was open for 4% of the time, Pallas kernels for 0%

profile of v5, /device:TPU:32, one launch (start us, length us, event | category | flops | bytes accessed | tf_op | source)
XLA Modules:
  0.0 237.4 jit_solution(15738524418415999016)
XLA Ops:
  0.6 0.0 copy-start.3
  0.6 1.6 broadcast_in_dim.22
  2.2 12.6 %all-to-all-start = ((bf16[8,16,1024]{2,1,0:T(8,128)(2,1)}), bf16[8,16,1024]{2,1,0:T(8,128)(2,1)S(1)}, u32[]{:S(2)}, u32[]{:S(2)}) async-start(bf16[8,16,1024]{2,1,0:T(8,128)(2,1)} %broadcast_in_dim.22), calls=%async_computation | async-start | bytes 524288 | tf_op jit(solution)/shard_map/all_to_all | solution.py:42
  14.8 1.9 collective-permute-start.1
  16.8 14.4 %all-to-all-done = bf16[8,16,1024]{2,1,0:T(8,128)(2,1)S(1)} async-done(((bf16[8,16,1024]{2,1,0:T(8,128)(2,1)}), bf16[8,16,1024]{2,1,0:T(8,128)(2,1)S(1)}, u32[]{:S(2)}, u32[]{:S(2)}) %all-to-all-start) | async-done | bytes 262176 | tf_op jit(solution)/shard_map/all_to_all | solution.py:42
  31.1 1.1 broadcast_in_dim.48
  32.2 4.3 %all-to-all-start.1 = ((bf16[4,128,1024]{2,1,0:T(8,128)(2,1)}), bf16[4,128,1024]{2,1,0:T(8,128)(2,1)S(1)}, u32[]{:S(2)}, u32[]{:S(2)}) async-start(bf16[4,128,1024]{2,1,0:T(8,128)(2,1)} %broadcast_in_dim.48), calls=%async_computation.1 | async-start | bytes 2097152 | tf_op jit(solution)/shard_map/all_to_all | solution.py:42
  36.5 0.0 collective-permute-done.1
  36.5 10.9 %all-to-all-done.1 = bf16[4,128,1024]{2,1,0:T(8,128)(2,1)S(1)} async-done(((bf16[4,128,1024]{2,1,0:T(8,128)(2,1)}), bf16[4,128,1024]{2,1,0:T(8,128)(2,1)S(1)}, u32[]{:S(2)}, u32[]{:S(2)}) %all-to-all-start.1) | async-done | bytes 1048608 | tf_op jit(solution)/shard_map/all_to_all | solution.py:42
  47.4 1.2 multiply_convert_fusion.1
  48.6 0.0 copy-start.4
  48.6 13.9 %all_to_all.40 = f16[4,192,512]{2,1,0:T(8,128)(2,1)S(1)} all-to-all(f16[4,192,512]{2,1,0:T(8,128)(2,1)S(1)} %bitcast.76), channel_id=1, replica_groups=mesh['x'=4,'zl'=8,'c'=2,'y'=4,'zh'=2] {'y'}, dimensions={0} | all-to-all | bytes 1572864 | tf_op jit(solution)/shard_map/all_to_all | solution.py:42
  62.5 0.3 fusion.13
  62.7 0.1 multiply_convert_fusion.3
  62.8 8.2 %collective-permute-start.2 = (f16[192,512]{1,0:T(8,128)(2,1)S(1)}, f16[192,512]{1,0:T(8,128)(2,1)S(1)}, u32[]{:S(2)}, u32[]{:S(2)}) collective-permute-start(f16[192,512]{1,0:T(8,128)(2,1)S(1)} %multiply_convert_fusion.3), channel_id=1, source_target_pairs={{0,1},{1,0},{2,3},{3,2},{4,5},{5,4},{6,7},{7,6},{8,9},{9,8},{10,11... | collective-permute-start | bytes 589832 | tf_op jit(solution)/shard_map/ppermute | solution.py:38
  71.1 0.0 copy-done.4
  71.1 1.9 collective-permute-start
  73.0 11.4 %collective-permute-done.2 = f16[192,512]{1,0:T(8,128)(2,1)S(1)} collective-permute-done((f16[192,512]{1,0:T(8,128)(2,1)S(1)}, f16[192,512]{1,0:T(8,128)(2,1)S(1)}, u32[]{:S(2)}, u32[]{:S(2)}) %collective-permute-start.2) | collective-permute-done | bytes 196640 | tf_op jit(solution)/shard_map/ppermute | solution.py:38
  84.4 0.1 fusion.26
  84.4 0.9 broadcast_in_dim.49
  85.4 3.5 %all-to-all-start.3 = ((bf16[4,192,512]{2,1,0:T(8,128)(2,1)}), bf16[4,192,512]{2,1,0:T(8,128)(2,1)S(1)}, u32[]{:S(2)}, u32[]{:S(2)}) async-start(bf16[4,192,512]{2,1,0:T(8,128)(2,1)} %broadcast_in_dim.49), calls=%async_computation.3 | async-start | bytes 1572864 | tf_op jit(solution)/shard_map/all_to_all | solution.py:42
  88.9 0.0 collective-permute-done
  88.9 9.4 %all-to-all-done.3 = bf16[4,192,512]{2,1,0:T(8,128)(2,1)S(1)} async-done(((bf16[4,192,512]{2,1,0:T(8,128)(2,1)}), bf16[4,192,512]{2,1,0:T(8,128)(2,1)S(1)}, u32[]{:S(2)}, u32[]{:S(2)}) %all-to-all-start.3) | async-done | bytes 786464 | tf_op jit(solution)/shard_map/all_to_all | solution.py:42
  98.3 2.3 multiply_convert_fusion
  100.7 3.5 %all-to-all-start.4 = ((f16[4,256,512]{2,1,0:T(8,128)(2,1)}), f16[4,256,512]{2,1,0:T(8,128)(2,1)S(1)}, u32[]{:S(2)}, u32[]{:S(2)}) async-start(f16[4,256,512]{2,1,0:T(8,128)(2,1)} %bitcast.7), calls=%async_computation.4 | async-start | bytes 2097152 | tf_op jit(solution)/shard_map/all_to_all | solution.py:42
  104.2 0.0 copy-start.1
  104.2 0.0 copy-start.2
  104.3 10.8 %all-to-all-done.4 = f16[4,256,512]{2,1,0:T(8,128)(2,1)S(1)} async-done(((f16[4,256,512]{2,1,0:T(8,128)(2,1)}), f16[4,256,512]{2,1,0:T(8,128)(2,1)S(1)}, u32[]{:S(2)}, u32[]{:S(2)}) %all-to-all-start.4) | async-done | bytes 1048608 | tf_op jit(solution)/shard_map/all_to_all | solution.py:42
  115.1 0.4 fusion.9
  115.4 0.8 multiply_convert_fusion.2
  116.2 19.8 %all-to-all-start.5 = ((f16[16,16,512]{2,1,0:T(8,128)(2,1)}), f16[16,16,512]{2,1,0:T(8,128)(2,1)S(1)}, u32[]{:S(2)}, u32[]{:S(2)}) async-start(f16[16,16,512]{2,1,0:T(8,128)(2,1)} %multiply_convert_fusion.2), calls=%async_computation.5 | async-start | bytes 524288 | tf_op jit(solution)/shard_map/all_to_all | solution.py:42
  136.0 0.8 fusion.4
  136.8 1.3 fusion.27
  138.1 2.1 collective-permute-start.4
  140.2 10.1 %all-to-all-done.5 = f16[16,16,512]{2,1,0:T(8,128)(2,1)S(1)} async-done(((f16[16,16,512]{2,1,0:T(8,128)(2,1)}), f16[16,16,512]{2,1,0:T(8,128)(2,1)S(1)}, u32[]{:S(2)}, u32[]{:S(2)}) %all-to-all-start.5) | async-done | bytes 262176 | tf_op jit(solution)/shard_map/all_to_all | solution.py:42
  150.3 0.1 abs_multiply_fusion.2
  150.5 0.1 divide_convert_fusion
  150.5 6.7 %collective-permute-start.3 = (bf16[16,1024]{1,0:T(8,128)(2,1)S(1)}, bf16[16,1024]{1,0:T(8,128)(2,1)S(1)}, u32[]{:S(2)}, u32[]{:S(2)}) collective-permute-start(bf16[16,1024]{1,0:T(8,128)(2,1)S(1)} %get-tuple-element.14), channel_id=1, source_target_pairs={{0,1},{1,0},{2,3},{3,2},{4,5},{5,4},{6,7},{7,6},{8,9},{9,8},{10,11... | collective-permute-start | bytes 98312 | tf_op jit(solution)/shard_map/ppermute | solution.py:38
  157.2 7.8 %collective-permute-done.3 = bf16[16,1024]{1,0:T(8,128)(2,1)S(1)} collective-permute-done((bf16[16,1024]{1,0:T(8,128)(2,1)S(1)}, bf16[16,1024]{1,0:T(8,128)(2,1)S(1)}, u32[]{:S(2)}, u32[]{:S(2)}) %collective-permute-start.3) | collective-permute-done | bytes 32800 | tf_op jit(solution)/shard_map/ppermute | solution.py:38
  165.1 0.7 broadcast_in_dim.50
  165.8 4.0 %all-to-all-start.6 = ((bf16[4,32,1024]{2,1,0:T(8,128)(2,1)}), bf16[4,32,1024]{2,1,0:T(8,128)(2,1)}, u32[]{:S(2)}, u32[]{:S(2)}) async-start(bf16[4,32,1024]{2,1,0:T(8,128)(2,1)} %broadcast_in_dim.50), calls=%async_computation.6 | async-start | bytes 524288 | tf_op jit(solution)/shard_map/all_to_all | solution.py:42
  169.9 0.0 collective-permute-done.4
  169.9 2.3 broadcast_select_fusion.1
  172.2 5.7 %all-to-all-done.6 = bf16[4,32,1024]{2,1,0:T(8,128)(2,1)} async-done(((bf16[4,32,1024]{2,1,0:T(8,128)(2,1)}), bf16[4,32,1024]{2,1,0:T(8,128)(2,1)}, u32[]{:S(2)}, u32[]{:S(2)}) %all-to-all-start.6) | async-done | bytes 262176 | tf_op jit(solution)/shard_map/all_to_all | solution.py:42
  178.0 2.7 %fusion.54 = (bf16[8,16,1024]{2,1,0:T(8,128)(2,1)S(1)}, f32[8,16,1024]{2,1,0:T(8,128)}) fusion(f32[8,16,1024]{2,1,0:T(8,128)} %param.9, bf16[8,16,1024]{2,1,0:T(8,128)(2,1)} %bitcast.12, bf16[512,1024]{1,0:T(8,128)(2,1)} %get-tuple-element.18, bf16[512,1024]{1,0:T(8,128)(2,1)S(1)} %get-tuple-element.17), kind=kOutput, calls=%fused_computation.96 | convolution fusion | flops 273022976 | bytes 3670016 | tf_op jit(solution)/shard_map/dot_general | solution.py:115
  180.6 6.7 %collective-permute-start.8 = (bf16[128,1024]{1,0:T(8,128)(2,1)S(1)}, bf16[128,1024]{1,0:T(8,128)(2,1)S(1)}, u32[]{:S(2)}, u32[]{:S(2)}) collective-permute-start(bf16[128,1024]{1,0:T(8,128)(2,1)S(1)} %bitcast.69), channel_id=1, source_target_pairs={{0,1},{1,0},{2,3},{3,2},{4,5},{5,4},{6,7},{7,6},{8,9},{9,8},{10,11... | collective-permute-start | bytes 786440 | tf_op jit(solution)/shard_map/ppermute | solution.py:38
  187.3 3.1 %collective-permute-start.7 = (bf16[128,1024]{1,0:T(8,128)(2,1)S(1)}, bf16[128,1024]{1,0:T(8,128)(2,1)S(1)}, u32[]{:S(2)}, u32[]{:S(2)}) collective-permute-start(bf16[128,1024]{1,0:T(8,128)(2,1)S(1)} %bitcast.70), channel_id=1, source_target_pairs={{0,6},{2,0},{4,2},{6,4},{1,7},{3,1},{5,3},{7,5},{8,14},{10,8},{12,... | collective-permute-start | bytes 786440 | tf_op jit(solution)/shard_map/ppermute | solution.py:122
  190.4 2.8 %collective-permute-start.6 = (bf16[128,1024]{1,0:T(8,128)(2,1)S(1)}, bf16[128,1024]{1,0:T(8,128)(2,1)S(1)}, u32[]{:S(2)}, u32[]{:S(2)}) collective-permute-start(bf16[128,1024]{1,0:T(8,128)(2,1)S(1)} %bitcast.71), channel_id=1, source_target_pairs={{0,2},{2,4},{4,6},{6,0},{1,3},{3,5},{5,7},{7,1},{8,10},{10,12},{12... | collective-permute-start | bytes 786440 | tf_op jit(solution)/shard_map/ppermute | solution.py:122
  193.2 2.5 %collective-permute-start.5 = (bf16[128,1024]{1,0:T(8,128)(2,1)S(1)}, bf16[128,1024]{1,0:T(8,128)(2,1)S(1)}, u32[]{:S(2)}, u32[]{:S(2)}) collective-permute-start(bf16[128,1024]{1,0:T(8,128)(2,1)S(1)} %bitcast.72), channel_id=1, source_target_pairs={{0,4},{2,6},{4,0},{6,2},{1,5},{3,7},{5,1},{7,3},{8,12},{10,14},{12... | collective-permute-start | bytes 786440 | tf_op jit(solution)/shard_map/ppermute | solution.py:122
  195.7 1.9 fusion.31
  197.6 0.7 slice_bitcast_fusion
  198.2 17.6 %collective-permute-done.8 = bf16[128,1024]{1,0:T(8,128)(2,1)S(1)} collective-permute-done((bf16[128,1024]{1,0:T(8,128)(2,1)S(1)}, bf16[128,1024]{1,0:T(8,128)(2,1)S(1)}, u32[]{:S(2)}, u32[]{:S(2)}) %collective-permute-start.8) | collective-permute-done | bytes 262176 | tf_op jit(solution)/shard_map/ppermute | solution.py:38
  215.9 0.0 collective-permute-done.7
  215.9 0.0 collective-permute-done.6
  215.9 0.0 collective-permute-done.5
  215.9 1.1 broadcast_in_dim.53
  217.0 3.5 %all-to-all-start.7 = ((bf16[4,128,1024]{2,1,0:T(8,128)(2,1)}), bf16[4,128,1024]{2,1,0:T(8,128)(2,1)S(1)}, u32[]{:S(2)}, u32[]{:S(2)}) async-start(bf16[4,128,1024]{2,1,0:T(8,128)(2,1)} %broadcast_in_dim.53), calls=%async_computation.7 | async-start | bytes 2097152 | tf_op jit(solution)/shard_map/all_to_all | solution.py:42
  220.7 0.1 constant_dynamic-slice_fusion
  220.8 0.3 broadcast_in_dim.51
  221.1 0.1 copy_dynamic-update-slice_fusion.1
  221.2 14.8 %all-to-all-done.7 = bf16[4,128,1024]{2,1,0:T(8,128)(2,1)S(1)} async-done(((bf16[4,128,1024]{2,1,0:T(8,128)(2,1)}), bf16[4,128,1024]{2,1,0:T(8,128)(2,1)S(1)}, u32[]{:S(2)}, u32[]{:S(2)}) %all-to-all-start.7) | async-done | bytes 1048608 | tf_op jit(solution)/shard_map/all_to_all | solution.py:42
  236.0 0.1 copy_dynamic-update-slice_fusion
  236.1 0.0 copy-start
  236.1 1.3 copy-done
  (20 shorter events, 0.2 us)
Async XLA Ops:
  0.6 46.8 %copy-start.3 = (bf16[384,1024]{1,0:T(8,128)(2,1)S(1)}, bf16[384,1024]{1,0:T(8,128)(2,1)}, u32[]{:S(2)}) copy-start(bf16[384,1024]{1,0:T(8,128)(2,1)} %param.6) | copy-start | bytes 2359300
  2.2 28.9 %all-to-all-start = ((bf16[8,16,1024]{2,1,0:T(8,128)(2,1)}), bf16[8,16,1024]{2,1,0:T(8,128)(2,1)S(1)}, u32[]{:S(2)}, u32[]{:S(2)}) async-start(bf16[8,16,1024]{2,1,0:T(8,128)(2,1)} %broadcast_in_dim.22), calls=%async_computation | async-start | bytes 524288 | tf_op jit(solution)/shard_map/all_to_all | solution.py:42
  14.8 21.7 %collective-permute-start.1 = (bf16[384,1024]{1,0:T(8,128)(2,1)}, bf16[384,1024]{1,0:T(8,128)(2,1)S(1)}, u32[]{:S(2)}, u32[]{:S(2)}) collective-permute-start(bf16[384,1024]{1,0:T(8,128)(2,1)} %param.6), channel_id=1, source_target_pairs={{0,8},{8,0},{1,9},{9,1},{2,10},{10,2},{3,11},{11,3},{4,12},{12,4},... | collective-permute-start | bytes 2359304 | tf_op jit(solution)/shard_map/ppermute | solution.py:38
  32.2 15.2 %all-to-all-start.1 = ((bf16[4,128,1024]{2,1,0:T(8,128)(2,1)}), bf16[4,128,1024]{2,1,0:T(8,128)(2,1)S(1)}, u32[]{:S(2)}, u32[]{:S(2)}) async-start(bf16[4,128,1024]{2,1,0:T(8,128)(2,1)} %broadcast_in_dim.48), calls=%async_computation.1 | async-start | bytes 2097152 | tf_op jit(solution)/shard_map/all_to_all | solution.py:42
  48.6 22.5 %copy-start.4 = (bf16[384,1024]{1,0:T(8,128)(2,1)S(1)}, bf16[384,1024]{1,0:T(8,128)(2,1)}, u32[]{:S(2)}) copy-start(bf16[384,1024]{1,0:T(8,128)(2,1)} %param.7) | copy-start | bytes 2359300
  62.8 21.5 %collective-permute-start.2 = (f16[192,512]{1,0:T(8,128)(2,1)S(1)}, f16[192,512]{1,0:T(8,128)(2,1)S(1)}, u32[]{:S(2)}, u32[]{:S(2)}) collective-permute-start(f16[192,512]{1,0:T(8,128)(2,1)S(1)} %multiply_convert_fusion.3), channel_id=1, source_target_pairs={{0,1},{1,0},{2,3},{3,2},{4,5},{5,4},{6,7},{7,6},{8,9},{9,8},{10,11... | collective-permute-start | bytes 589832 | tf_op jit(solution)/shard_map/ppermute | solution.py:38
  71.1 17.8 %collective-permute-start = (bf16[384,1024]{1,0:T(8,128)(2,1)S(1)}, bf16[384,1024]{1,0:T(8,128)(2,1)S(1)}, u32[]{:S(2)}, u32[]{:S(2)}) collective-permute-start(bf16[384,1024]{1,0:T(8,128)(2,1)S(1)} %copy-done.4), channel_id=1, source_target_pairs={{0,8},{8,0},{1,9},{9,1},{2,10},{10,2},{3,11},{11,3},{4,12},{12,4},... | collective-permute-start | bytes 2359304 | tf_op jit(solution)/shard_map/ppermute | solution.py:38
  85.4 13.0 %all-to-all-start.3 = ((bf16[4,192,512]{2,1,0:T(8,128)(2,1)}), bf16[4,192,512]{2,1,0:T(8,128)(2,1)S(1)}, u32[]{:S(2)}, u32[]{:S(2)}) async-start(bf16[4,192,512]{2,1,0:T(8,128)(2,1)} %broadcast_in_dim.49), calls=%async_computation.3 | async-start | bytes 1572864 | tf_op jit(solution)/shard_map/all_to_all | solution.py:42
  100.7 14.4 %all-to-all-start.4 = ((f16[4,256,512]{2,1,0:T(8,128)(2,1)}), f16[4,256,512]{2,1,0:T(8,128)(2,1)S(1)}, u32[]{:S(2)}, u32[]{:S(2)}) async-start(f16[4,256,512]{2,1,0:T(8,128)(2,1)} %bitcast.7), calls=%async_computation.4 | async-start | bytes 2097152 | tf_op jit(solution)/shard_map/all_to_all | solution.py:42
  104.2 32.6 %copy-start.1 = (f32[1,16,1024]{2,1,0:T(8,128)S(1)}, f32[1,16,1024]{2,1,0:T(8,128)}, u32[]{:S(2)}) copy-start(f32[1,16,1024]{2,1,0:T(8,128)} %param.11) | copy-start | bytes 196612
  104.2 32.6 %copy-start.2 = (f32[1,16,1024]{2,1,0:T(8,128)S(1)}, f32[1,16,1024]{2,1,0:T(8,128)}, u32[]{:S(2)}) copy-start(f32[1,16,1024]{2,1,0:T(8,128)} %param.10) | copy-start | bytes 196612
  116.2 34.1 %all-to-all-start.5 = ((f16[16,16,512]{2,1,0:T(8,128)(2,1)}), f16[16,16,512]{2,1,0:T(8,128)(2,1)S(1)}, u32[]{:S(2)}, u32[]{:S(2)}) async-start(f16[16,16,512]{2,1,0:T(8,128)(2,1)} %multiply_convert_fusion.2), calls=%async_computation.5 | async-start | bytes 524288 | tf_op jit(solution)/shard_map/all_to_all | solution.py:42
  138.1 31.7 %collective-permute-start.4 = (bf16[512,1024]{1,0:T(8,128)(2,1)S(1)}, bf16[512,1024]{1,0:T(8,128)(2,1)}, u32[]{:S(2)}, u32[]{:S(2)}) collective-permute-start(bf16[512,1024]{1,0:T(8,128)(2,1)S(1)} %bitcast.62), channel_id=1, source_target_pairs={{0,8},{8,0},{1,9},{9,1},{2,10},{10,2},{3,11},{11,3},{4,12},{12,4},... | collective-permute-start | bytes 3145736 | tf_op jit(solution)/shard_map/ppermute | solution.py:38
  150.5 14.5 %collective-permute-start.3 = (bf16[16,1024]{1,0:T(8,128)(2,1)S(1)}, bf16[16,1024]{1,0:T(8,128)(2,1)S(1)}, u32[]{:S(2)}, u32[]{:S(2)}) collective-permute-start(bf16[16,1024]{1,0:T(8,128)(2,1)S(1)} %get-tuple-element.14), channel_id=1, source_target_pairs={{0,1},{1,0},{2,3},{3,2},{4,5},{5,4},{6,7},{7,6},{8,9},{9,8},{10,11... | collective-permute-start | bytes 98312 | tf_op jit(solution)/shard_map/ppermute | solution.py:38
  165.8 12.1 %all-to-all-start.6 = ((bf16[4,32,1024]{2,1,0:T(8,128)(2,1)}), bf16[4,32,1024]{2,1,0:T(8,128)(2,1)}, u32[]{:S(2)}, u32[]{:S(2)}) async-start(bf16[4,32,1024]{2,1,0:T(8,128)(2,1)} %broadcast_in_dim.50), calls=%async_computation.6 | async-start | bytes 524288 | tf_op jit(solution)/shard_map/all_to_all | solution.py:42
  180.6 35.2 %collective-permute-start.8 = (bf16[128,1024]{1,0:T(8,128)(2,1)S(1)}, bf16[128,1024]{1,0:T(8,128)(2,1)S(1)}, u32[]{:S(2)}, u32[]{:S(2)}) collective-permute-start(bf16[128,1024]{1,0:T(8,128)(2,1)S(1)} %bitcast.69), channel_id=1, source_target_pairs={{0,1},{1,0},{2,3},{3,2},{4,5},{5,4},{6,7},{7,6},{8,9},{9,8},{10,11... | collective-permute-start | bytes 786440 | tf_op jit(solution)/shard_map/ppermute | solution.py:38
  187.3 28.6 %collective-permute-start.7 = (bf16[128,1024]{1,0:T(8,128)(2,1)S(1)}, bf16[128,1024]{1,0:T(8,128)(2,1)S(1)}, u32[]{:S(2)}, u32[]{:S(2)}) collective-permute-start(bf16[128,1024]{1,0:T(8,128)(2,1)S(1)} %bitcast.70), channel_id=1, source_target_pairs={{0,6},{2,0},{4,2},{6,4},{1,7},{3,1},{5,3},{7,5},{8,14},{10,8},{12,... | collective-permute-start | bytes 786440 | tf_op jit(solution)/shard_map/ppermute | solution.py:122
  190.4 25.5 %collective-permute-start.6 = (bf16[128,1024]{1,0:T(8,128)(2,1)S(1)}, bf16[128,1024]{1,0:T(8,128)(2,1)S(1)}, u32[]{:S(2)}, u32[]{:S(2)}) collective-permute-start(bf16[128,1024]{1,0:T(8,128)(2,1)S(1)} %bitcast.71), channel_id=1, source_target_pairs={{0,2},{2,4},{4,6},{6,0},{1,3},{3,5},{5,7},{7,1},{8,10},{10,12},{12... | collective-permute-start | bytes 786440 | tf_op jit(solution)/shard_map/ppermute | solution.py:122
  193.2 22.7 %collective-permute-start.5 = (bf16[128,1024]{1,0:T(8,128)(2,1)S(1)}, bf16[128,1024]{1,0:T(8,128)(2,1)S(1)}, u32[]{:S(2)}, u32[]{:S(2)}) collective-permute-start(bf16[128,1024]{1,0:T(8,128)(2,1)S(1)} %bitcast.72), channel_id=1, source_target_pairs={{0,4},{2,6},{4,0},{6,2},{1,5},{3,7},{5,1},{7,3},{8,12},{10,14},{12... | collective-permute-start | bytes 786440 | tf_op jit(solution)/shard_map/ppermute | solution.py:122
  217.0 19.0 %all-to-all-start.7 = ((bf16[4,128,1024]{2,1,0:T(8,128)(2,1)}), bf16[4,128,1024]{2,1,0:T(8,128)(2,1)S(1)}, u32[]{:S(2)}, u32[]{:S(2)}) async-start(bf16[4,128,1024]{2,1,0:T(8,128)(2,1)} %broadcast_in_dim.53), calls=%async_computation.7 | async-start | bytes 2097152 | tf_op jit(solution)/shard_map/all_to_all | solution.py:42
  236.1 1.3 copy-start

commit v6 on v4

--- a/solution.py
+++ b/solution.py
@@ -121,11 +121,11 @@
     tiled = (Y, Y * ZH, cols // ROWS, ROWS, feats)
     here = lax.axis_index("y")
     parts = [block_forward] + [
-        lax.ppermute(block_forward, "y", [(i, (i + d) % Y) for i in range(Y)]) for d in (2, 1, 3)
+        lax.ppermute(block_forward, "y", [(i, (i + d) % Y) for i in range(Y)]) for d in (1, 3, 2)
     ]
     far_block = swap(block_forward, "zh")
     *parts, far_block = lax.optimization_barrier((*parts, far_block))
-    by_step = [parts[0], parts[2], parts[1], parts[3]]
+    by_step = [parts[0], parts[1], parts[3], parts[2]]
     stacked = jnp.stack(by_step[::-1] + by_step[::-1], 0)
     own = lax.dynamic_slice_in_dim(stacked, Y - 1 - here, Y, 0)
     theirs = gather(far_block, "y", Y)

time: 238 us -> 238 us (level)
  no operation moved by 1% of the time
where the time goes in v6:
time: 238 us; the launch traced here: 237 us
  waiting for transfers between devices  112 us (47%)
  starting transfers between devices  86.9 us (37%)
  blocking collectives  13.9 us (6%)
  matrix products  9.31 us (4%)
  local copies, waits for them, and re-layouts  8.15 us (3%)
  other arithmetic  4.97 us (2%)
    all_to_all x7, waiting for transfers between devices, exchange(): return lax.all_to_all(value, axis, 0, 0)  76.2 us
    all_to_all x7, starting transfers between devices, exchange(): return lax.all_to_all(value, axis, 0, 0)  50.6 us
    ppermute x6, waiting for transfers between devices, swap(): return lax.ppermute(value, axis, SWAP)  36.2 us
    ppermute x6, starting transfers between devices, swap(): return lax.ppermute(value, axis, SWAP)  27.3 us
    all_to_all x1, blocking collectives, exchange(): return lax.all_to_all(value, axis, 0, 0)  13.9 us
    ppermute x3, starting transfers between devices, on_device(): lax.ppermute(block_forward, 'y', [(i, (i + d) % Y) for i in range(Y)])  8.98 us
    broadcast_in_dim x5, local copies, waits for them, and re-layouts, gather(): return exchange(jnp.broadcast_to(value[None], (count, *value.shape)), axis)  5.43 us
  transfers between devices with their start and end apart: 16, of which 10 were waited for; matrix products, arithmetic and copies ran while one was open for 5% of the time, Pallas kernels for 0%

profile of v6, /device:TPU:32, one launch (start us, length us, event | category | flops | bytes accessed | tf_op | source)
XLA Modules:
  0.0 236.7 jit_solution(552633964456735150)
XLA Ops:
  0.6 0.0 copy-start.3
  0.6 1.6 broadcast_in_dim.22
  2.2 12.6 %all-to-all-start = ((bf16[8,16,1024]{2,1,0:T(8,128)(2,1)}), bf16[8,16,1024]{2,1,0:T(8,128)(2,1)S(1)}, u32[]{:S(2)}, u32[]{:S(2)}) async-start(bf16[8,16,1024]{2,1,0:T(8,128)(2,1)} %broadcast_in_dim.22), calls=%async_computation | async-start | bytes 524288 | tf_op jit(solution)/shard_map/all_to_all | solution.py:42
  14.8 1.9 collective-permute-start.1
  16.8 14.4 %all-to-all-done = bf16[8,16,1024]{2,1,0:T(8,128)(2,1)S(1)} async-done(((bf16[8,16,1024]{2,1,0:T(8,128)(2,1)}), bf16[8,16,1024]{2,1,0:T(8,128)(2,1)S(1)}, u32[]{:S(2)}, u32[]{:S(2)}) %all-to-all-start) | async-done | bytes 262176 | tf_op jit(solution)/shard_map/all_to_all | solution.py:42
  31.1 1.1 broadcast_in_dim.48
  32.2 4.3 %all-to-all-start.1 = ((bf16[4,128,1024]{2,1,0:T(8,128)(2,1)}), bf16[4,128,1024]{2,1,0:T(8,128)(2,1)S(1)}, u32[]{:S(2)}, u32[]{:S(2)}) async-start(bf16[4,128,1024]{2,1,0:T(8,128)(2,1)} %broadcast_in_dim.48), calls=%async_computation.1 | async-start | bytes 2097152 | tf_op jit(solution)/shard_map/all_to_all | solution.py:42
  36.5 0.0 collective-permute-done.1
  36.5 10.9 %all-to-all-done.1 = bf16[4,128,1024]{2,1,0:T(8,128)(2,1)S(1)} async-done(((bf16[4,128,1024]{2,1,0:T(8,128)(2,1)}), bf16[4,128,1024]{2,1,0:T(8,128)(2,1)S(1)}, u32[]{:S(2)}, u32[]{:S(2)}) %all-to-all-start.1) | async-done | bytes 1048608 | tf_op jit(solution)/shard_map/all_to_all | solution.py:42
  47.4 1.2 multiply_convert_fusion.1
  48.6 0.0 copy-start.4
  48.6 13.9 %all_to_all.40 = f16[4,192,512]{2,1,0:T(8,128)(2,1)S(1)} all-to-all(f16[4,192,512]{2,1,0:T(8,128)(2,1)S(1)} %bitcast.78), channel_id=1, replica_groups=mesh['x'=4,'zl'=8,'c'=2,'y'=4,'zh'=2] {'y'}, dimensions={0} | all-to-all | bytes 1572864 | tf_op jit(solution)/shard_map/all_to_all | solution.py:42
  62.5 0.3 fusion.13
  62.7 0.1 multiply_convert_fusion.3
  62.8 8.2 %collective-permute-start.2 = (f16[192,512]{1,0:T(8,128)(2,1)S(1)}, f16[192,512]{1,0:T(8,128)(2,1)S(1)}, u32[]{:S(2)}, u32[]{:S(2)}) collective-permute-start(f16[192,512]{1,0:T(8,128)(2,1)S(1)} %multiply_convert_fusion.3), channel_id=1, source_target_pairs={{0,1},{1,0},{2,3},{3,2},{4,5},{5,4},{6,7},{7,6},{8,9},{9,8},{10,11... | collective-permute-start | bytes 589832 | tf_op jit(solution)/shard_map/ppermute | solution.py:38
  71.1 0.0 copy-done.4
  71.1 1.9 collective-permute-start
  73.0 11.4 %collective-permute-done.2 = f16[192,512]{1,0:T(8,128)(2,1)S(1)} collective-permute-done((f16[192,512]{1,0:T(8,128)(2,1)S(1)}, f16[192,512]{1,0:T(8,128)(2,1)S(1)}, u32[]{:S(2)}, u32[]{:S(2)}) %collective-permute-start.2) | collective-permute-done | bytes 196640 | tf_op jit(solution)/shard_map/ppermute | solution.py:38
  84.4 0.1 fusion.26
  84.4 0.9 broadcast_in_dim.49
  85.4 3.5 %all-to-all-start.3 = ((bf16[4,192,512]{2,1,0:T(8,128)(2,1)}), bf16[4,192,512]{2,1,0:T(8,128)(2,1)S(1)}, u32[]{:S(2)}, u32[]{:S(2)}) async-start(bf16[4,192,512]{2,1,0:T(8,128)(2,1)} %broadcast_in_dim.49), calls=%async_computation.3 | async-start | bytes 1572864 | tf_op jit(solution)/shard_map/all_to_all | solution.py:42
  88.9 0.0 collective-permute-done
  88.9 9.4 %all-to-all-done.3 = bf16[4,192,512]{2,1,0:T(8,128)(2,1)S(1)} async-done(((bf16[4,192,512]{2,1,0:T(8,128)(2,1)}), bf16[4,192,512]{2,1,0:T(8,128)(2,1)S(1)}, u32[]{:S(2)}, u32[]{:S(2)}) %all-to-all-start.3) | async-done | bytes 786464 | tf_op jit(solution)/shard_map/all_to_all | solution.py:42
  98.3 2.3 multiply_convert_fusion
  100.7 3.5 %all-to-all-start.4 = ((f16[4,256,512]{2,1,0:T(8,128)(2,1)}), f16[4,256,512]{2,1,0:T(8,128)(2,1)S(1)}, u32[]{:S(2)}, u32[]{:S(2)}) async-start(f16[4,256,512]{2,1,0:T(8,128)(2,1)} %bitcast.7), calls=%async_computation.4 | async-start | bytes 2097152 | tf_op jit(solution)/shard_map/all_to_all | solution.py:42
  104.2 0.0 copy-start.1
  104.2 0.0 copy-start.2
  104.3 1.9 collective-permute-start.4
  106.2 8.8 %all-to-all-done.4 = f16[4,256,512]{2,1,0:T(8,128)(2,1)S(1)} async-done(((f16[4,256,512]{2,1,0:T(8,128)(2,1)}), f16[4,256,512]{2,1,0:T(8,128)(2,1)S(1)}, u32[]{:S(2)}, u32[]{:S(2)}) %all-to-all-start.4) | async-done | bytes 1048608 | tf_op jit(solution)/shard_map/all_to_all | solution.py:42
  115.1 0.4 fusion.9
  115.4 0.8 multiply_convert_fusion.2
  116.2 19.8 %all-to-all-start.5 = ((f16[16,16,512]{2,1,0:T(8,128)(2,1)}), f16[16,16,512]{2,1,0:T(8,128)(2,1)S(1)}, u32[]{:S(2)}, u32[]{:S(2)}) async-start(f16[16,16,512]{2,1,0:T(8,128)(2,1)} %multiply_convert_fusion.2), calls=%async_computation.5 | async-start | bytes 524288 | tf_op jit(solution)/shard_map/all_to_all | solution.py:42
  136.0 0.8 fusion.4
  136.8 1.3 fusion.27
  138.1 12.2 %all-to-all-done.5 = f16[16,16,512]{2,1,0:T(8,128)(2,1)S(1)} async-done(((f16[16,16,512]{2,1,0:T(8,128)(2,1)}), f16[16,16,512]{2,1,0:T(8,128)(2,1)S(1)}, u32[]{:S(2)}, u32[]{:S(2)}) %all-to-all-start.5) | async-done | bytes 262176 | tf_op jit(solution)/shard_map/all_to_all | solution.py:42
  150.3 0.1 abs_multiply_fusion.2
  150.5 0.1 divide_convert_fusion
  150.5 6.7 %collective-permute-start.3 = (bf16[16,1024]{1,0:T(8,128)(2,1)S(1)}, bf16[16,1024]{1,0:T(8,128)(2,1)S(1)}, u32[]{:S(2)}, u32[]{:S(2)}) collective-permute-start(bf16[16,1024]{1,0:T(8,128)(2,1)S(1)} %get-tuple-element.14), channel_id=1, source_target_pairs={{0,1},{1,0},{2,3},{3,2},{4,5},{5,4},{6,7},{7,6},{8,9},{9,8},{10,11... | collective-permute-start | bytes 98312 | tf_op jit(solution)/shard_map/ppermute | solution.py:38
  157.2 7.8 %collective-permute-done.3 = bf16[16,1024]{1,0:T(8,128)(2,1)S(1)} collective-permute-done((bf16[16,1024]{1,0:T(8,128)(2,1)S(1)}, bf16[16,1024]{1,0:T(8,128)(2,1)S(1)}, u32[]{:S(2)}, u32[]{:S(2)}) %collective-permute-start.3) | collective-permute-done | bytes 32800 | tf_op jit(solution)/shard_map/ppermute | solution.py:38
  165.1 0.7 broadcast_in_dim.50
  165.8 3.4 %all-to-all-start.6 = ((bf16[4,32,1024]{2,1,0:T(8,128)(2,1)}), bf16[4,32,1024]{2,1,0:T(8,128)(2,1)S(1)}, u32[]{:S(2)}, u32[]{:S(2)}) async-start(bf16[4,32,1024]{2,1,0:T(8,128)(2,1)} %broadcast_in_dim.50), calls=%async_computation.6 | async-start | bytes 524288 | tf_op jit(solution)/shard_map/all_to_all | solution.py:42
  169.2 0.0 collective-permute-done.4
  169.2 2.3 broadcast_select_fusion.1
  171.6 5.6 %all-to-all-done.6 = bf16[4,32,1024]{2,1,0:T(8,128)(2,1)S(1)} async-done(((bf16[4,32,1024]{2,1,0:T(8,128)(2,1)}), bf16[4,32,1024]{2,1,0:T(8,128)(2,1)S(1)}, u32[]{:S(2)}, u32[]{:S(2)}) %all-to-all-start.6) | async-done | bytes 262176 | tf_op jit(solution)/shard_map/all_to_all | solution.py:42
  177.3 2.6 %fusion.54 = (bf16[8,16,1024]{2,1,0:T(8,128)(2,1)S(1)}, f32[8,16,1024]{2,1,0:T(8,128)}) fusion(f32[8,16,1024]{2,1,0:T(8,128)} %param.9, bf16[8,16,1024]{2,1,0:T(8,128)(2,1)S(1)} %bitcast.79, bf16[512,1024]{1,0:T(8,128)(2,1)} %get-tuple-element.18, bf16[512,1024]{1,0:T(8,128)(2,1)S(1)} %get-tuple-element.17), kind=kOutput, calls=%fused_computation.97 | convolution fusion | flops 273022976 | bytes 3670016 | tf_op jit(solution)/shard_map/dot_general | solution.py:117
  179.9 6.7 %collective-permute-start.8 = (bf16[128,1024]{1,0:T(8,128)(2,1)S(1)}, bf16[128,1024]{1,0:T(8,128)(2,1)S(1)}, u32[]{:S(2)}, u32[]{:S(2)}) collective-permute-start(bf16[128,1024]{1,0:T(8,128)(2,1)S(1)} %bitcast.71), channel_id=1, source_target_pairs={{0,1},{1,0},{2,3},{3,2},{4,5},{5,4},{6,7},{7,6},{8,9},{9,8},{10,11... | collective-permute-start | bytes 786440 | tf_op jit(solution)/shard_map/ppermute | solution.py:38
  186.6 2.5 %collective-permute-start.7 = (bf16[128,1024]{1,0:T(8,128)(2,1)S(1)}, bf16[128,1024]{1,0:T(8,128)(2,1)S(1)}, u32[]{:S(2)}, u32[]{:S(2)}) collective-permute-start(bf16[128,1024]{1,0:T(8,128)(2,1)S(1)} %bitcast.72), channel_id=1, source_target_pairs={{0,4},{2,6},{4,0},{6,2},{1,5},{3,7},{5,1},{7,3},{8,12},{10,14},{12... | collective-permute-start | bytes 786440 | tf_op jit(solution)/shard_map/ppermute | solution.py:124
  189.0 4.6 %collective-permute-start.6 = (bf16[128,1024]{1,0:T(8,128)(2,1)S(1)}, bf16[128,1024]{1,0:T(8,128)(2,1)S(1)}, u32[]{:S(2)}, u32[]{:S(2)}) collective-permute-start(bf16[128,1024]{1,0:T(8,128)(2,1)S(1)} %bitcast.73), channel_id=1, source_target_pairs={{0,6},{2,0},{4,2},{6,4},{1,7},{3,1},{5,3},{7,5},{8,14},{10,8},{12,... | collective-permute-start | bytes 786440 | tf_op jit(solution)/shard_map/ppermute | solution.py:124
  193.6 1.9 collective-permute-start.5
  195.6 1.9 fusion.31
  197.4 0.7 slice_bitcast_fusion
  198.1 17.0 %collective-permute-done.8 = bf16[128,1024]{1,0:T(8,128)(2,1)S(1)} collective-permute-done((bf16[128,1024]{1,0:T(8,128)(2,1)S(1)}, bf16[128,1024]{1,0:T(8,128)(2,1)S(1)}, u32[]{:S(2)}, u32[]{:S(2)}) %collective-permute-start.8) | collective-permute-done | bytes 262176 | tf_op jit(solution)/shard_map/ppermute | solution.py:38
  215.1 0.0 collective-permute-done.7
  215.1 0.0 collective-permute-done.6
  215.1 0.0 collective-permute-done.5
  215.1 1.1 broadcast_in_dim.53
  216.2 3.5 %all-to-all-start.7 = ((bf16[4,128,1024]{2,1,0:T(8,128)(2,1)}), bf16[4,128,1024]{2,1,0:T(8,128)(2,1)S(1)}, u32[]{:S(2)}, u32[]{:S(2)}) async-start(bf16[4,128,1024]{2,1,0:T(8,128)(2,1)} %broadcast_in_dim.53), calls=%async_computation.7 | async-start | bytes 2097152 | tf_op jit(solution)/shard_map/all_to_all | solution.py:42
  220.0 0.1 constant_dynamic-slice_fusion
  220.0 0.3 broadcast_in_dim.51
  220.3 0.1 copy_dynamic-update-slice_fusion.1
  220.4 14.8 %all-to-all-done.7 = bf16[4,128,1024]{2,1,0:T(8,128)(2,1)S(1)} async-done(((bf16[4,128,1024]{2,1,0:T(8,128)(2,1)}), bf16[4,128,1024]{2,1,0:T(8,128)(2,1)S(1)}, u32[]{:S(2)}, u32[]{:S(2)}) %all-to-all-start.7) | async-done | bytes 1048608 | tf_op jit(solution)/shard_map/all_to_all | solution.py:42
  235.2 0.1 copy_dynamic-update-slice_fusion
  235.4 0.0 copy-start
  235.4 1.3 copy-done
  (21 shorter events, 0.3 us)
Async XLA Ops:
  0.6 46.8 %copy-start.3 = (bf16[384,1024]{1,0:T(8,128)(2,1)S(1)}, bf16[384,1024]{1,0:T(8,128)(2,1)}, u32[]{:S(2)}) copy-start(bf16[384,1024]{1,0:T(8,128)(2,1)} %param.6) | copy-start | bytes 2359300
  2.2 28.9 %all-to-all-start = ((bf16[8,16,1024]{2,1,0:T(8,128)(2,1)}), bf16[8,16,1024]{2,1,0:T(8,128)(2,1)S(1)}, u32[]{:S(2)}, u32[]{:S(2)}) async-start(bf16[8,16,1024]{2,1,0:T(8,128)(2,1)} %broadcast_in_dim.22), calls=%async_computation | async-start | bytes 524288 | tf_op jit(solution)/shard_map/all_to_all | solution.py:42
  14.8 21.7 %collective-permute-start.1 = (bf16[384,1024]{1,0:T(8,128)(2,1)}, bf16[384,1024]{1,0:T(8,128)(2,1)S(1)}, u32[]{:S(2)}, u32[]{:S(2)}) collective-permute-start(bf16[384,1024]{1,0:T(8,128)(2,1)} %param.6), channel_id=1, source_target_pairs={{0,8},{8,0},{1,9},{9,1},{2,10},{10,2},{3,11},{11,3},{4,12},{12,4},... | collective-permute-start | bytes 2359304 | tf_op jit(solution)/shard_map/ppermute | solution.py:38
  32.2 15.2 %all-to-all-start.1 = ((bf16[4,128,1024]{2,1,0:T(8,128)(2,1)}), bf16[4,128,1024]{2,1,0:T(8,128)(2,1)S(1)}, u32[]{:S(2)}, u32[]{:S(2)}) async-start(bf16[4,128,1024]{2,1,0:T(8,128)(2,1)} %broadcast_in_dim.48), calls=%async_computation.1 | async-start | bytes 2097152 | tf_op jit(solution)/shard_map/all_to_all | solution.py:42
  48.6 22.5 %copy-start.4 = (bf16[384,1024]{1,0:T(8,128)(2,1)S(1)}, bf16[384,1024]{1,0:T(8,128)(2,1)}, u32[]{:S(2)}) copy-start(bf16[384,1024]{1,0:T(8,128)(2,1)} %param.7) | copy-start | bytes 2359300
  62.8 21.5 %collective-permute-start.2 = (f16[192,512]{1,0:T(8,128)(2,1)S(1)}, f16[192,512]{1,0:T(8,128)(2,1)S(1)}, u32[]{:S(2)}, u32[]{:S(2)}) collective-permute-start(f16[192,512]{1,0:T(8,128)(2,1)S(1)} %multiply_convert_fusion.3), channel_id=1, source_target_pairs={{0,1},{1,0},{2,3},{3,2},{4,5},{5,4},{6,7},{7,6},{8,9},{9,8},{10,11... | collective-permute-start | bytes 589832 | tf_op jit(solution)/shard_map/ppermute | solution.py:38
  71.1 17.8 %collective-permute-start = (bf16[384,1024]{1,0:T(8,128)(2,1)S(1)}, bf16[384,1024]{1,0:T(8,128)(2,1)S(1)}, u32[]{:S(2)}, u32[]{:S(2)}) collective-permute-start(bf16[384,1024]{1,0:T(8,128)(2,1)S(1)} %copy-done.4), channel_id=1, source_target_pairs={{0,8},{8,0},{1,9},{9,1},{2,10},{10,2},{3,11},{11,3},{4,12},{12,4},... | collective-permute-start | bytes 2359304 | tf_op jit(solution)/shard_map/ppermute | solution.py:38
  85.4 13.0 %all-to-all-start.3 = ((bf16[4,192,512]{2,1,0:T(8,128)(2,1)}), bf16[4,192,512]{2,1,0:T(8,128)(2,1)S(1)}, u32[]{:S(2)}, u32[]{:S(2)}) async-start(bf16[4,192,512]{2,1,0:T(8,128)(2,1)} %broadcast_in_dim.49), calls=%async_computation.3 | async-start | bytes 1572864 | tf_op jit(solution)/shard_map/all_to_all | solution.py:42
  100.7 14.4 %all-to-all-start.4 = ((f16[4,256,512]{2,1,0:T(8,128)(2,1)}), f16[4,256,512]{2,1,0:T(8,128)(2,1)S(1)}, u32[]{:S(2)}, u32[]{:S(2)}) async-start(f16[4,256,512]{2,1,0:T(8,128)(2,1)} %bitcast.7), calls=%async_computation.4 | async-start | bytes 2097152 | tf_op jit(solution)/shard_map/all_to_all | solution.py:42
  104.2 32.6 %copy-start.1 = (f32[1,16,1024]{2,1,0:T(8,128)S(1)}, f32[1,16,1024]{2,1,0:T(8,128)}, u32[]{:S(2)}) copy-start(f32[1,16,1024]{2,1,0:T(8,128)} %param.11) | copy-start | bytes 196612
  104.2 32.6 %copy-start.2 = (f32[1,16,1024]{2,1,0:T(8,128)S(1)}, f32[1,16,1024]{2,1,0:T(8,128)}, u32[]{:S(2)}) copy-start(f32[1,16,1024]{2,1,0:T(8,128)} %param.10) | copy-start | bytes 196612
  104.3 64.9 %collective-permute-start.4 = (bf16[512,1024]{1,0:T(8,128)(2,1)S(1)}, bf16[512,1024]{1,0:T(8,128)(2,1)}, u32[]{:S(2)}, u32[]{:S(2)}) collective-permute-start(bf16[512,1024]{1,0:T(8,128)(2,1)S(1)} %bitcast.63), channel_id=1, source_target_pairs={{0,8},{8,0},{1,9},{9,1},{2,10},{10,2},{3,11},{11,3},{4,12},{12,4},... | collective-permute-start | bytes 3145736 | tf_op jit(solution)/shard_map/ppermute | solution.py:38
  116.2 34.1 %all-to-all-start.5 = ((f16[16,16,512]{2,1,0:T(8,128)(2,1)}), f16[16,16,512]{2,1,0:T(8,128)(2,1)S(1)}, u32[]{:S(2)}, u32[]{:S(2)}) async-start(f16[16,16,512]{2,1,0:T(8,128)(2,1)} %multiply_convert_fusion.2), calls=%async_computation.5 | async-start | bytes 524288 | tf_op jit(solution)/shard_map/all_to_all | solution.py:42
  150.5 14.5 %collective-permute-start.3 = (bf16[16,1024]{1,0:T(8,128)(2,1)S(1)}, bf16[16,1024]{1,0:T(8,128)(2,1)S(1)}, u32[]{:S(2)}, u32[]{:S(2)}) collective-permute-start(bf16[16,1024]{1,0:T(8,128)(2,1)S(1)} %get-tuple-element.14), channel_id=1, source_target_pairs={{0,1},{1,0},{2,3},{3,2},{4,5},{5,4},{6,7},{7,6},{8,9},{9,8},{10,11... | collective-permute-start | bytes 98312 | tf_op jit(solution)/shard_map/ppermute | solution.py:38
  165.8 11.4 %all-to-all-start.6 = ((bf16[4,32,1024]{2,1,0:T(8,128)(2,1)}), bf16[4,32,1024]{2,1,0:T(8,128)(2,1)S(1)}, u32[]{:S(2)}, u32[]{:S(2)}) async-start(bf16[4,32,1024]{2,1,0:T(8,128)(2,1)} %broadcast_in_dim.50), calls=%async_computation.6 | async-start | bytes 524288 | tf_op jit(solution)/shard_map/all_to_all | solution.py:42
  179.9 35.2 %collective-permute-start.8 = (bf16[128,1024]{1,0:T(8,128)(2,1)S(1)}, bf16[128,1024]{1,0:T(8,128)(2,1)S(1)}, u32[]{:S(2)}, u32[]{:S(2)}) collective-permute-start(bf16[128,1024]{1,0:T(8,128)(2,1)S(1)} %bitcast.71), channel_id=1, source_target_pairs={{0,1},{1,0},{2,3},{3,2},{4,5},{5,4},{6,7},{7,6},{8,9},{9,8},{10,11... | collective-permute-start | bytes 786440 | tf_op jit(solution)/shard_map/ppermute | solution.py:38
  186.6 28.5 %collective-permute-start.7 = (bf16[128,1024]{1,0:T(8,128)(2,1)S(1)}, bf16[128,1024]{1,0:T(8,128)(2,1)S(1)}, u32[]{:S(2)}, u32[]{:S(2)}) collective-permute-start(bf16[128,1024]{1,0:T(8,128)(2,1)S(1)} %bitcast.72), channel_id=1, source_target_pairs={{0,4},{2,6},{4,0},{6,2},{1,5},{3,7},{5,1},{7,3},{8,12},{10,14},{12... | collective-permute-start | bytes 786440 | tf_op jit(solution)/shard_map/ppermute | solution.py:124
  189.0 26.1 %collective-permute-start.6 = (bf16[128,1024]{1,0:T(8,128)(2,1)S(1)}, bf16[128,1024]{1,0:T(8,128)(2,1)S(1)}, u32[]{:S(2)}, u32[]{:S(2)}) collective-permute-start(bf16[128,1024]{1,0:T(8,128)(2,1)S(1)} %bitcast.73), channel_id=1, source_target_pairs={{0,6},{2,0},{4,2},{6,4},{1,7},{3,1},{5,3},{7,5},{8,14},{10,8},{12,... | collective-permute-start | bytes 786440 | tf_op jit(solution)/shard_map/ppermute | solution.py:124
  193.6 21.5 %collective-permute-start.5 = (bf16[128,1024]{1,0:T(8,128)(2,1)S(1)}, bf16[128,1024]{1,0:T(8,128)(2,1)S(1)}, u32[]{:S(2)}, u32[]{:S(2)}) collective-permute-start(bf16[128,1024]{1,0:T(8,128)(2,1)S(1)} %bitcast.74), channel_id=1, source_target_pairs={{0,2},{2,4},{4,6},{6,0},{1,3},{3,5},{5,7},{7,1},{8,10},{10,12},{12... | collective-permute-start | bytes 786440 | tf_op jit(solution)/shard_map/ppermute | solution.py:124
  216.2 19.0 %all-to-all-start.7 = ((bf16[4,128,1024]{2,1,0:T(8,128)(2,1)}), bf16[4,128,1024]{2,1,0:T(8,128)(2,1)S(1)}, u32[]{:S(2)}, u32[]{:S(2)}) async-start(bf16[4,128,1024]{2,1,0:T(8,128)(2,1)} %broadcast_in_dim.53), calls=%async_computation.7 | async-start | bytes 2097152 | tf_op jit(solution)/shard_map/all_to_all | solution.py:42
  235.4 1.3 copy-start
